TPU v7x, 32 devices: a whole 2x2x4 slice. The times are simulated.
32 devices in a mesh: row: 4 (over y, core), seq: 8 (over z, x).
Axes of the slice: x: 2, y: 2, z: 4, core: 2. Of those that a mesh axis runs over, the one named last changes fastest.
Arguments:
- inputs: bfloat16 [4, 1024, 2048], P('row', 'seq'), may hold values from -6 to 6
- lengths: int32 [4, 2], P('row'), may hold values from 352 to 672, as said below
- w_query: bfloat16 [2048, 2048], P(('row', 'seq')), may hold values from -0.1875 to 0.1875
- w_key: bfloat16 [2048, 2048], P(('row', 'seq')), may hold values from -0.1875 to 0.1875
- w_value: bfloat16 [2048, 2048], P(('row', 'seq')), may hold values from -0.125 to 0.125
- w_out: bfloat16 [2048, 2048], P(('row', 'seq')), may hold values from -2.5 to 2.5
- gain_attn: bfloat16 [2048], P(('row', 'seq')), may hold values from 0.5 to 1.5
- w_gate: bfloat16 [2048, 8192], P(('row', 'seq')), may hold values from -0.125 to 0.125
- w_up: bfloat16 [2048, 8192], P(('row', 'seq')), may hold values from -0.125 to 0.125
- w_down: bfloat16 [8192, 2048], P(('row', 'seq')), may hold values from -0.0625 to 0.0625
- gain_mlp: bfloat16 [2048], P(('row', 'seq')), may hold values from 0.5 to 1.5
- cotangent: bfloat16 [4, 1024, 2048], P('row', 'seq'), may hold values from -6 to 6
Outputs:
- output: bfloat16 [4, 1024, 2048], P('row', 'seq')
- input_grad: float32 [4, 1024, 2048], P('row', 'seq')
- grad_query: float32 [2048, 2048], P(('row', 'seq'))
- grad_key: float32 [2048, 2048], P(('row', 'seq'))
- grad_value: float32 [2048, 2048], P(('row', 'seq'))
- grad_out: float32 [2048, 2048], P(('row', 'seq'))
- grad_gain_attn: float32 [2048], P(('row', 'seq'))
- grad_gate: float32 [2048, 8192], P(('row', 'seq'))
- grad_up: float32 [2048, 8192], P(('row', 'seq'))
- grad_down: float32 [8192, 2048], P(('row', 'seq'))
- grad_gain_mlp: float32 [2048], P(('row', 'seq'))
Inputs may be any that keep to these rules, and one draw needn't show every extreme that they name: The lengths of a row add up to 1024 and are multiples of 16.
All inputs are finite; a program needn't handle non-finite values.
Results may differ from a plain program's by a relative error of at most 0.012.
The roundings to bfloat16 on the way count: a program that leaves them out, or rounds other values in their place, can miss the bound.
Values may be sent and summed in bfloat16 or wider, within the bound.
A program may use at most 512 MiB of HBM per device.

v0:
```python
import functools

import jax
import jax.numpy as jnp
from jax import lax
from jax.experimental import pallas as pl
from jax.experimental.pallas import tpu as pltpu
from jax.sharding import PartitionSpec as P

HEADS = 16


EPSILON = 1e-05


def layout(lengths_row, places, block_rows, block_count):
    unit_counts = lengths_row // (2 * block_count)
    span_sizes = 2 * unit_counts
    offsets = jnp.cumsum(span_sizes) - span_sizes
    device = places // block_rows
    within_block = places - device * block_rows
    inside = (
        (within_block[:, None] >= offsets[None, :])
        & (within_block[:, None] < (offsets + span_sizes)[None, :])
    ).astype(jnp.int32)
    numbers = jnp.arange(lengths_row.shape[0], dtype=jnp.int32)
    segment = jnp.sum(inside * numbers[None, :], axis=1)
    unit_of = jnp.sum(inside * unit_counts[None, :], axis=1)
    begins = jnp.sum(inside * offsets[None, :], axis=1)
    length_of = jnp.sum(inside * lengths_row[None, :], axis=1)
    within = within_block - begins
    position = jnp.where(
        within < unit_of,
        device * unit_of + within,
        (2 * block_count - 1 - device) * unit_of + within - unit_of,
    )
    return (segment, position, length_of)


def rms_norm(values, gain):
    return values * lax.rsqrt(jnp.mean(values * values, axis=-1, keepdims=True) + EPSILON) * gain


def sigmoid_terms(query_heads, query_meta, key_heads, key_meta):
    query_segment, query_position, query_length = query_meta
    key_segment, key_position, unused_length = key_meta
    scores = jnp.einsum(
        "qhd,khd->hqk", query_heads, key_heads, preferred_element_type=jnp.float32
    ) * query_heads.shape[2] ** (-0.5)
    scores = scores - jnp.log(query_length.astype(jnp.float32))[None, :, None]
    allowed = (query_segment[:, None] == key_segment[None, :]) & (
        key_position[None, :] <= query_position[:, None]
    )
    return jnp.where(allowed[None], jax.nn.sigmoid(scores), 0.0)


def pair_terms(query_heads, query_meta, grad_heads, key_heads, key_meta, value_heads):
    sig_terms = sigmoid_terms(query_heads, query_meta, key_heads, key_meta)
    slopes = jnp.einsum("qhd,khd->hqk", grad_heads, value_heads, preferred_element_type=jnp.float32)
    score_grad = (slopes * sig_terms * (1.0 - sig_terms)).astype(jnp.bfloat16)
    return (sig_terms.astype(jnp.bfloat16), score_grad)


def by_blocks(step_fn, running, pieces, block_rows):
    size_total = pieces[0].shape[0]
    part_rows = 4 * block_rows
    block_count = size_total // part_rows

    def turn_over(step_number, carried):
        sub_pieces = tuple(
            (
                lax.dynamic_slice_in_dim(member, step_number * part_rows, part_rows, 0)
                for member in pieces
            )
        )
        return step_fn(carried, sub_pieces, step_number * part_rows)

    return lax.fori_loop(0, block_count, turn_over, running)


def gathered_local(
    inputs,
    lengths,
    w_query,
    w_key,
    w_value,
    w_out,
    gain_attn,
    w_gate,
    w_up,
    w_down,
    gain_mlp,
    cotangent,
):
    residual = inputs[0].astype(jnp.float32)
    tokens_here = residual.shape[0]
    model_width = residual.shape[1]
    head_size = model_width // HEADS
    score_scale = head_size ** (-0.5)
    block_total = lax.axis_size("seq")
    lengths_row = lengths[0]
    places = lax.axis_index("seq") * tokens_here + jnp.arange(tokens_here, dtype=jnp.int32)
    own_meta = layout(lengths_row, places, tokens_here, block_total)

    def meta_at(start_row, row_count):
        return layout(
            lengths_row,
            start_row + jnp.arange(row_count, dtype=jnp.int32),
            tokens_here,
            block_total,
        )

    def heads_of(matrix):
        return matrix.reshape(matrix.shape[0], HEADS, head_size)

    query_full, key_full, value_full, out_full, gain_one = (
        lax.all_gather(w_query, ("row", "seq"), axis=0, tiled=True),
        lax.all_gather(w_key, ("row", "seq"), axis=0, tiled=True),
        lax.all_gather(w_value, ("row", "seq"), axis=0, tiled=True),
        lax.all_gather(w_out, ("row", "seq"), axis=0, tiled=True),
        lax.all_gather(gain_attn, ("row", "seq"), axis=0, tiled=True),
    )
    gain_one_f = gain_one.astype(jnp.float32)
    normed = rms_norm(residual, gain_one_f).astype(jnp.bfloat16)
    queries = jnp.dot(normed, query_full, preferred_element_type=jnp.float32).astype(jnp.bfloat16)
    key_rows = jnp.dot(normed, key_full, preferred_element_type=jnp.float32).astype(jnp.bfloat16)
    value_rows = jnp.dot(normed, value_full, preferred_element_type=jnp.float32).astype(
        jnp.bfloat16
    )
    query_heads = heads_of(queries)

    def forward_step(running, pieces, start_row):
        key_piece, value_piece = pieces
        sig_terms = sigmoid_terms(
            query_heads, own_meta, heads_of(key_piece), meta_at(start_row, key_piece.shape[0])
        ).astype(jnp.bfloat16)
        added = jnp.einsum(
            "hqk,khd->qhd", sig_terms, heads_of(value_piece), preferred_element_type=jnp.float32
        )
        return running + added.reshape(tokens_here, model_width)

    attended = by_blocks(
        forward_step,
        jnp.zeros((tokens_here, model_width), jnp.float32),
        (
            lax.all_gather(key_rows, "seq", axis=0, tiled=True),
            lax.all_gather(value_rows, "seq", axis=0, tiled=True),
        ),
        tokens_here,
    )
    attended_low = attended.astype(jnp.bfloat16)
    middle = residual + jnp.dot(attended_low, out_full, preferred_element_type=jnp.float32)
    gate_full, up_full, down_full, gain_two = (
        lax.all_gather(w_gate, ("row", "seq"), axis=0, tiled=True),
        lax.all_gather(w_up, ("row", "seq"), axis=0, tiled=True),
        lax.all_gather(w_down, ("row", "seq"), axis=0, tiled=True),
        lax.all_gather(gain_mlp, ("row", "seq"), axis=0, tiled=True),
    )
    gain_two_f = gain_two.astype(jnp.float32)
    normed_mlp = rms_norm(middle, gain_two_f).astype(jnp.bfloat16)
    gate_vals = jnp.dot(normed_mlp, gate_full, preferred_element_type=jnp.float32)
    up_vals = jnp.dot(normed_mlp, up_full, preferred_element_type=jnp.float32)
    gated_prod, gated_back = jax.vjp(
        lambda gate_in, up_in: jax.nn.silu(gate_in) * up_in, gate_vals, up_vals
    )
    hidden = gated_prod.astype(jnp.bfloat16)
    output = (middle + jnp.dot(hidden, down_full, preferred_element_type=jnp.float32)).astype(
        jnp.bfloat16
    )
    upstream_low = cotangent[0]
    upstream = upstream_low.astype(jnp.float32)
    gate_full, up_full, down_full, gain_two = (
        lax.all_gather(w_gate, ("row", "seq"), axis=0, tiled=True),
        lax.all_gather(w_up, ("row", "seq"), axis=0, tiled=True),
        lax.all_gather(w_down, ("row", "seq"), axis=0, tiled=True),
        lax.all_gather(gain_mlp, ("row", "seq"), axis=0, tiled=True),
    )
    gain_two_f = gain_two.astype(jnp.float32)
    grad_down = jnp.dot(hidden.T, upstream_low, preferred_element_type=jnp.float32)
    shared_down = lax.psum_scatter(grad_down, ("row", "seq"), scatter_dimension=0, tiled=True)
    hidden_grad = jnp.dot(upstream_low, down_full.T, preferred_element_type=jnp.float32)
    gate_grad, up_grad = gated_back(hidden_grad)
    gate_low = gate_grad.astype(jnp.bfloat16)
    up_low = up_grad.astype(jnp.bfloat16)
    grad_gate = jnp.dot(normed_mlp.T, gate_low, preferred_element_type=jnp.float32)
    shared_gate = lax.psum_scatter(grad_gate, ("row", "seq"), scatter_dimension=0, tiled=True)
    normed_grad = jnp.dot(gate_low, gate_full.T, preferred_element_type=jnp.float32) + jnp.dot(
        up_low, up_full.T, preferred_element_type=jnp.float32
    )
    unused_mid, second_back = jax.vjp(rms_norm, middle, gain_two_f)
    middle_part, gain_two_grad = second_back(normed_grad)
    middle_grad = upstream + middle_part
    grad_up = jnp.dot(normed_mlp.T, up_low, preferred_element_type=jnp.float32)
    shared_up, shared_gain_two = (
        lax.psum_scatter(grad_up, ("row", "seq"), scatter_dimension=0, tiled=True),
        lax.psum_scatter(gain_two_grad, ("row", "seq"), scatter_dimension=0, tiled=True),
    )
    query_full, key_full, value_full, out_full, gain_one = (
        lax.all_gather(w_query, ("row", "seq"), axis=0, tiled=True),
        lax.all_gather(w_key, ("row", "seq"), axis=0, tiled=True),
        lax.all_gather(w_value, ("row", "seq"), axis=0, tiled=True),
        lax.all_gather(w_out, ("row", "seq"), axis=0, tiled=True),
        lax.all_gather(gain_attn, ("row", "seq"), axis=0, tiled=True),
    )
    gain_one_f = gain_one.astype(jnp.float32)
    branch_low = middle_grad.astype(jnp.bfloat16)
    grad_out = jnp.dot(attended_low.T, branch_low, preferred_element_type=jnp.float32)
    attended_grad = jnp.dot(branch_low, out_full.T, preferred_element_type=jnp.float32).astype(
        jnp.bfloat16
    )
    grad_heads = heads_of(attended_grad)
    key_heads_own = heads_of(key_rows)
    value_heads_own = heads_of(value_rows)

    def query_step(running, pieces, start_row):
        key_piece, value_piece = pieces
        key_piece_heads = heads_of(key_piece)
        unused_terms, score_grad = pair_terms(
            query_heads,
            own_meta,
            grad_heads,
            key_piece_heads,
            meta_at(start_row, key_piece.shape[0]),
            heads_of(value_piece),
        )
        added = jnp.einsum(
            "hqk,khd->qhd", score_grad, key_piece_heads, preferred_element_type=jnp.float32
        )
        return running + added.reshape(tokens_here, model_width) * score_scale

    start_value = jnp.zeros((tokens_here, model_width), jnp.float32)
    folded = by_blocks(
        query_step,
        start_value,
        (
            lax.all_gather(key_rows, "seq", axis=0, tiled=True),
            lax.all_gather(value_rows, "seq", axis=0, tiled=True),
        ),
        tokens_here,
    )

    def key_step(running, pieces, start_row):
        key_sum, value_sum = running
        query_piece, grad_piece = pieces
        row_count = query_piece.shape[0]
        query_piece_heads = heads_of(query_piece)
        grad_piece_heads = heads_of(grad_piece)
        sig_low, score_grad = pair_terms(
            query_piece_heads,
            meta_at(start_row, row_count),
            grad_piece_heads,
            key_heads_own,
            own_meta,
            value_heads_own,
        )
        key_add = jnp.einsum(
            "hqk,qhd->khd", score_grad, query_piece_heads, preferred_element_type=jnp.float32
        )
        value_add = jnp.einsum(
            "hqk,qhd->khd", sig_low, grad_piece_heads, preferred_element_type=jnp.float32
        )
        return (
            key_sum + key_add.reshape(tokens_here, model_width) * score_scale,
            value_sum + value_add.reshape(tokens_here, model_width),
        )

    empty_rows = jnp.zeros((tokens_here, model_width), jnp.float32)
    key_grad, value_grad = by_blocks(
        key_step,
        (empty_rows, empty_rows),
        (
            lax.all_gather(queries, "seq", axis=0, tiled=True),
            lax.all_gather(attended_grad, "seq", axis=0, tiled=True),
        ),
        tokens_here,
    )
    query_low = folded.astype(jnp.bfloat16)
    key_low = key_grad.astype(jnp.bfloat16)
    value_low = value_grad.astype(jnp.bfloat16)
    grad_query = jnp.dot(normed.T, query_low, preferred_element_type=jnp.float32)
    grad_key = jnp.dot(normed.T, key_low, preferred_element_type=jnp.float32)
    grad_value = jnp.dot(normed.T, value_low, preferred_element_type=jnp.float32)
    normed_back = jnp.dot(query_low, query_full.T, preferred_element_type=jnp.float32)
    normed_back = normed_back + jnp.dot(key_low, key_full.T, preferred_element_type=jnp.float32)
    normed_back = normed_back + jnp.dot(value_low, value_full.T, preferred_element_type=jnp.float32)
    unused_first, first_back = jax.vjp(rms_norm, residual, gain_one_f)
    residual_part, gain_one_grad = first_back(normed_back)
    input_grad = middle_grad + residual_part
    shared_query, shared_key, shared_value, shared_out, shared_gain_one = (
        lax.psum_scatter(grad_query, ("row", "seq"), scatter_dimension=0, tiled=True),
        lax.psum_scatter(grad_key, ("row", "seq"), scatter_dimension=0, tiled=True),
        lax.psum_scatter(grad_value, ("row", "seq"), scatter_dimension=0, tiled=True),
        lax.psum_scatter(grad_out, ("row", "seq"), scatter_dimension=0, tiled=True),
        lax.psum_scatter(gain_one_grad, ("row", "seq"), scatter_dimension=0, tiled=True),
    )
    return (
        output[None],
        input_grad[None],
        shared_query,
        shared_key,
        shared_value,
        shared_out,
        shared_gain_one,
        shared_gate,
        shared_up,
        shared_down,
        shared_gain_two,
    )


MESH = pl.DeviceIdType.MESH
VMEM_BYTES = 62 * 1024 * 1024


class Place:
    def __init__(self, row_count, seq_count):
        self.row_count, self.seq_count = row_count, seq_count
        self.r, self.s = lax.axis_index("row"), lax.axis_index("seq")
        self.n_hi = seq_count // 2
        self.hi, self.lo = self.s // 2, lax.rem(self.s, 2)
        self.r_core = self.r + 1 - 2 * lax.rem(self.r, 2)
        self.r_y = lax.rem(self.r + 2, 4)
        self.r_far = lax.rem(self.r_core + 2, 4)
        self.side = (self.r, self.s + 1 - 2 * self.lo)
        self.up = (self.r, self.s + 2)
        self.down = (self.r, self.s - 2)
        self.core = (self.r_core, self.s)
        self.y = (self.r_y, self.s)
        self.has_up = self.hi < self.n_hi - 1
        self.has_down = self.hi > 0

    def peer(self, step):
        return lax.rem(self.s + step, self.seq_count)

    def chain(self):
        return [(None, self.side), (self.has_up, self.up), (self.has_down, self.down)]

    def peers(self):
        return [(None, (self.r, self.peer(step))) for step in range(1, self.seq_count)]

    def rows(self):
        return [(None, self.core), (None, self.y)]


def greet(devices):
    barrier = pltpu.get_barrier_semaphore()
    total = 0
    for condition, device in devices:
        if condition is None:
            pl.semaphore_signal(barrier, inc=1, device_id=device, device_id_type=MESH)
            total = total + 1
        else:

            @pl.when(condition)
            def _(device=device):
                pl.semaphore_signal(barrier, inc=1, device_id=device, device_id_type=MESH)

            total = total + condition.astype(jnp.int32)
    pl.semaphore_wait(barrier, total)


class Sems:
    def __init__(self, ref):
        self.ref, self.used = ref, 0

    def take(self, count):
        base = self.used
        self.used += count
        assert self.used <= self.ref.shape[0], self.used
        return lambda index: self.ref.at[base + index]


def push(source, target, send, recv, device):
    pltpu.make_async_remote_copy(
        src_ref=source, dst_ref=target, send_sem=send, recv_sem=recv, device_id=device, device_id_type=MESH
    ).start()


def settle(ref, sem):
    pltpu.make_async_copy(ref, ref, sem).wait()


def no_op(block):
    return None


class SeqGather:
    def __init__(self, place, sems, source, at, arrived=no_op):
        self.p, self.source, self.at, self.arrived = place, source, at, arrived
        self.own_done = False
        n = place.n_hi
        self.own, self.up, self.down = sems.take(1), sems.take(n), sems.take(n)
        self.side, self.recv = sems.take(n), sems.take(2 * n)

    def start(self):
        p, s = self.p, self.p.s
        pltpu.make_async_copy(self.source, self.at(s), self.own(0)).start()

        @pl.when(p.has_up)
        def _():
            push(self.source, self.at(s), self.up(0), self.recv(s), p.up)

        @pl.when(p.has_down)
        def _():
            push(self.source, self.at(s), self.down(0), self.recv(s), p.down)

        push(self.source, self.at(s), self.side(p.hi), self.recv(s), p.side)

    def step(self, k):
        p = self.p

        @pl.when(p.hi >= k)
        def _():
            block = p.s - 2 * k
            settle(self.at(block), self.recv(block))

            @pl.when(p.has_up)
            def _():
                push(self.at(block), self.at(block), self.up(k), self.recv(block), p.up)

            push(self.at(block), self.at(block), self.side(p.hi - k), self.recv(block), p.side)
            self.arrived(block)

        @pl.when(p.hi + k < p.n_hi)
        def _():
            block = p.s + 2 * k
            settle(self.at(block), self.recv(block))

            @pl.when(p.has_down)
            def _():
                push(self.at(block), self.at(block), self.down(k), self.recv(block), p.down)

            push(self.at(block), self.at(block), self.side(p.hi + k), self.recv(block), p.side)
            self.arrived(block)

    def aside(self, k):
        p = self.p
        if k == 0:
            block = 2 * p.hi + 1 - p.lo
            settle(self.at(block), self.recv(block))
            self.arrived(block)
            return

        @pl.when(p.hi >= k)
        def _():
            block = 2 * (p.hi - k) + 1 - p.lo
            settle(self.at(block), self.recv(block))
            self.arrived(block)

        @pl.when(p.hi + k < p.n_hi)
        def _():
            block = 2 * (p.hi + k) + 1 - p.lo
            settle(self.at(block), self.recv(block))
            self.arrived(block)

    def settle_own(self):
        settle(self.at(self.p.s), self.own(0))
        self.own_done = True

    def finish(self):
        p = self.p
        if not self.own_done:
            self.settle_own()
        for k in range(p.n_hi):

            @pl.when(p.has_up & (p.hi >= k))
            def _():
                settle(self.source, self.up(k))

            @pl.when(p.has_down & (p.hi + k < p.n_hi))
            def _():
                settle(self.source, self.down(k))

            settle(self.source, self.side(k))


class SeqExchange:
    def __init__(self, place, sems, piece, at, arrived=no_op):
        self.p, self.piece, self.at, self.arrived = place, piece, at, arrived
        self.own_done = False
        n = place.seq_count
        self.own, self.send, self.recv = sems.take(1), sems.take(n), sems.take(n)

    def start_own(self):
        s = self.p.s
        pltpu.make_async_copy(self.piece(s), self.at(s), self.own(0)).start()

    def start(self):
        p, s = self.p, self.p.s
        self.start_own()
        for step in range(1, p.seq_count):
            t = p.peer(step)
            push(self.piece(t), self.at(s), self.send(step), self.recv(s), (p.r, t))

    def step(self, step):
        block = self.p.peer(self.p.seq_count - step)
        settle(self.at(block), self.recv(block))
        self.arrived(block)

    def finish(self):
        p = self.p
        settle(self.at(p.s), self.own(0))
        for step in range(1, p.seq_count):
            settle(self.at(p.s), self.send(step))


class PartExchange(SeqExchange):
    def __init__(self, place, sems, parts, at, arrived=no_op):
        super().__init__(place, sems, None, at, arrived)
        self.parts = parts

    def start_own(self):
        s = self.p.s
        for source, target in self.parts(s):
            pltpu.make_async_copy(source, target, self.own(0)).start()

    def start(self):
        p, s = self.p, self.p.s
        self.start_own()
        for step in range(1, p.seq_count):
            t = p.peer(step)
            for source, target in self.parts(t):
                push(source, target, self.send(step), self.recv(s), (p.r, t))

    def settle_own(self):
        settle(self.at(self.p.s), self.own(0))
        self.own_done = True

    def finish(self):
        p = self.p
        if not self.own_done:
            self.settle_own()
        for step in range(1, p.seq_count):
            settle(self.at(p.s), self.send(step))


class RowForward:
    def __init__(self, place, sems, blocks, at):
        self.p, self.at, self.blocks = place, at, blocks
        self.core, self.y, self.far = sems.take(blocks), sems.take(blocks), sems.take(blocks)
        self.from_core, self.from_y, self.from_far = sems.take(blocks), sems.take(blocks), sems.take(blocks)

    def forward(self, block, source=None):
        p = self.p
        source = self.at(p.r, block) if source is None else source
        push(source, self.at(p.r, block), self.y(block), self.from_y(block), p.y)
        push(source, self.at(p.r, block), self.core(block), self.from_core(block), p.core)

    def relay(self, block):
        p = self.p
        settle(self.at(p.r_y, block), self.from_y(block))
        push(self.at(p.r_y, block), self.at(p.r_y, block), self.far(block), self.from_far(block), p.core)

    def finish(self):
        p = self.p
        for block in range(self.blocks):
            settle(self.at(p.r_core, block), self.from_core(block))
            settle(self.at(p.r_far, block), self.from_far(block))
            settle(self.at(p.r, block), self.core(block))
            settle(self.at(p.r, block), self.y(block))
            settle(self.at(p.r_y, block), self.far(block))


def add_into(target, *sources):
    @pl.loop(0, target.shape[0] // 16)
    def _(tile):
        rows = pl.ds(pl.multiple_of(tile * 16, 16), 16)
        total = sources[0][rows, :].astype(jnp.float32)
        for source in sources[1:]:
            total = total + source[rows, :].astype(jnp.float32)
        target[rows, :] = total.astype(target.dtype)


def add_small(target, *sources):
    total = sources[0][...].astype(jnp.float32)
    for source in sources[1:]:
        total = total + source[...].astype(jnp.float32)
    target[...] = total.astype(target.dtype)


class SeqReduce:
    def __init__(self, place, sems, at, side_slot, chain_slot, target, add=add_into):
        self.p, self.at, self.add, self.target = place, at, add, target
        self.side_slot, self.chain_slot = side_slot, chain_slot
        n = place.n_hi
        self.side, self.from_side = sems.take(n), sems.take(n)
        self.send, self.recv = sems.take(n), sems.take(2 * n)

    def above_slot(self, block, hi):
        return self.chain_slot(jnp.where(block == hi, self.p.n_hi, block))

    def turn(self, t):
        p = self.p
        n, hi = p.n_hi, p.hi
        low = jnp.where(t < n - 1 - hi, n - 1 - t, t - (n - 1 - hi))
        high = jnp.where(t < hi, t, n - 1 - (t - hi))
        return jnp.where(hi < n // 2, low, high)

    def start(self, t):
        p, block = self.p, self.turn(t)
        push(self.at(2 * block + 1 - p.lo), self.side_slot(block), self.side(block), self.from_side(block), p.side)

    def step(self, t):
        p, n, block = self.p, self.p.n_hi, self.turn(t)
        mine, got = self.at(2 * block + p.lo), self.side_slot(block)
        settle(got, self.from_side(block))
        if t == n - 1:
            return self.close()

        @pl.when(block > p.hi)
        def _():
            @pl.when(p.has_down)
            def _():
                settle(got, self.recv(block))
                self.add(got, mine, got, self.chain_slot(block))

            @pl.when(jnp.logical_not(p.has_down))
            def _():
                self.add(got, mine, got)

            push(got, self.chain_slot(block), self.send(block), self.recv(block), p.up)

        @pl.when(block < p.hi)
        def _():
            @pl.when(p.has_up)
            def _():
                settle(got, self.recv(n + block))
                self.add(got, mine, got, self.above_slot(block, p.hi))

            @pl.when(jnp.logical_not(p.has_up))
            def _():
                self.add(got, mine, got)

            push(got, self.above_slot(block, p.hi - 1), self.send(block), self.recv(n + block), p.down)

    def close(self):
        p, n, hi = self.p, self.p.n_hi, self.p.hi
        mine, got = self.at(p.s), self.side_slot(hi)
        below, above = self.chain_slot(hi), self.above_slot(hi, hi)

        @pl.when(p.has_down)
        def _():
            settle(got, self.recv(hi))

        @pl.when(p.has_up)
        def _():
            settle(got, self.recv(n + hi))

        @pl.when(p.has_down & p.has_up)
        def _():
            self.add(self.target, mine, got, below, above)

        @pl.when(p.has_down & jnp.logical_not(p.has_up))
        def _():
            self.add(self.target, mine, got, below)

        @pl.when(jnp.logical_not(p.has_down))
        def _():
            self.add(self.target, mine, got, above)

    def finish(self):
        p = self.p
        for block in range(p.n_hi):
            settle(self.side_slot(block), self.side(block))

            @pl.when(p.hi != block)
            def _():
                settle(self.side_slot(block), self.send(block))


class RowReduce:
    def __init__(self, place, sems, blocks, at, core_slot, y_slot, target, add=add_into, own=None):
        self.p, self.at, self.add, self.target = place, at, add, target
        self.own = own or (lambda w, b: at((place.r_y, place.r)[w], b))
        self.core_slot, self.y_slot, self.blocks = core_slot, y_slot, blocks
        self.send, self.recv = sems.take(2 * blocks), sems.take(2 * blocks)
        self.y, self.from_y = sems.take(blocks), sems.take(blocks)

    def start_far(self, block):
        p = self.p
        push(self.at(p.r_far, block), self.core_slot(0, block), self.send(block), self.recv(block), p.core)

    def start_core(self, block):
        p, n = self.p, self.blocks
        push(self.at(p.r_core, block), self.core_slot(1, block), self.send(n + block), self.recv(n + block), p.core)

    def start(self, block):
        self.start_far(block)
        self.start_core(block)

    def step(self, block):
        p = self.p
        got = self.core_slot(0, block)
        settle(got, self.recv(block))
        self.add(got, self.own(0, block), got)
        push(got, self.y_slot(block), self.y(block), self.from_y(block), p.y)

    def close(self, block):
        p = self.p
        settle(self.core_slot(1, block), self.recv(self.blocks + block))
        settle(self.y_slot(block), self.from_y(block))
        self.add(self.target(block), self.own(1, block), self.core_slot(1, block), self.y_slot(block))

    def finish(self):
        n = self.blocks
        for block in range(n):
            settle(self.core_slot(0, block), self.send(block))
            settle(self.core_slot(1, block), self.send(n + block))
            settle(self.core_slot(0, block), self.y(block))


def columns(ref, index, width):
    return ref.at[:, pl.ds(pl.multiple_of(index * width, width), width)]


def call(kernel, shapes, ident, args, spaces, out_spaces, scratch, sems):
    return pl.pallas_call(
        kernel,
        out_shape=shapes,
        in_specs=[pl.BlockSpec(memory_space=space) for space in spaces],
        out_specs=jax.tree.map(lambda space: pl.BlockSpec(memory_space=space), out_spaces),
        scratch_shapes=list(scratch) + [pltpu.SemaphoreType.DMA((sems,))],
        compiler_params=pltpu.CompilerParams(
            collective_id=ident, has_side_effects=True, vmem_limit_bytes=VMEM_BYTES
        ),
    )(*args)


def shape_of(dims, dtype=jnp.bfloat16):
    return jax.ShapeDtypeStruct(dims, dtype)


def nt(left, right):
    return lax.dot_general(left, right, (((1,), (1,)), ((), ())), preferred_element_type=jnp.float32)


def tn(left, right):
    return lax.dot_general(left, right, (((0,), (0,)), ((), ())), preferred_element_type=jnp.float32)


def nn(left, right):
    return lax.dot_general(left, right, (((1,), (0,)), ((), ())), preferred_element_type=jnp.float32)


def rows_at(index, count):
    return pl.ds(pl.multiple_of(index * count, count), count)


def norm_rows(source, target, gain):
    @pl.loop(0, source.shape[0] // 16)
    def _(tile):
        rows = rows_at(tile, 16)
        values = source[rows, :].astype(jnp.float32)
        target[rows, :] = rms_norm(values, gain[...]).astype(target.dtype)


def attention(qkv, attended, key_place, query_low, query_high, shift, turned, head, head_size):
    tokens, own_width = attended.shape
    scale = head_size ** (-0.5)
    keys_step = 256
    lanes = pl.ds(head * head_size, head_size)
    key_lanes = pl.ds(own_width + head * head_size, head_size)
    value_lanes = pl.ds(2 * own_width + head * head_size, head_size)
    turned[...] = jnp.zeros_like(turned)

    @pl.loop(0, tokens // keys_step)
    def _(step):
        rows = rows_at(step, keys_step)
        places = key_place[rows, :]
        allowed = (places >= query_low[...]) & (places <= query_high[...])
        scores = nt(qkv[rows, key_lanes], qkv[:, lanes]) * scale - shift[...]
        sig = jnp.where(allowed, jax.nn.sigmoid(scores), 0.0).astype(jnp.bfloat16)
        turned[...] += nn(qkv[rows, value_lanes].T, sig)

    attended[:, lanes] = turned[...].T.astype(jnp.bfloat16)


def forward_kernel(
    rows,
    seqs,
    head_size,
    x,
    g,
    wquery,
    wkey,
    wvalue,
    wgate,
    wup,
    wdown,
    wout,
    gains,
    key_place,
    query_low,
    query_high,
    shift,
    gs,
    vgu,
    vdown,
    vout,
    h2,
    vqkv,
    hn,
    qkv,
    attended,
    middle,
    gain_rows_out,
    xs,
    vgains,
    heads,
    turned,
    out_held,
    h2_own,
    copies,
    sems,
):
    p, pool = Place(rows, seqs), Sems(sems)
    greet(p.peers() + p.rows())
    tokens, width = x.shape
    half = tokens // 2
    own_width = heads.shape[1]
    deep = wout.shape[0]
    down_blocks = vdown.shape[1]

    def part(source, target, c, arrived=no_op):
        piece = pl.ds(c * half, half)
        return SeqGather(p, pool, source.at[piece], lambda b: target.at[b, piece], arrived)

    def norm_half(c):
        def run(b):
            start = pl.multiple_of(b * tokens + c * half, half)
            norm_rows(xs.at[b, pl.ds(c * half, half)], hn.at[pl.ds(start, half), :], gain_rows_out.at[0:1, :])

        return run

    qkv_rows = RowForward(p, pool, seqs, lambda r, b: vqkv.at[r, b])
    gu_rows = RowForward(p, pool, seqs, lambda r, b: vgu.at[r, b])
    down_fwd = RowForward(p, pool, down_blocks, lambda r, b: vdown.at[r, b])
    out_rows = RowForward(p, pool, seqs, lambda r, b: vout.at[r, b])
    gain_rows = RowForward(p, pool, 1, lambda r, b: vgains.at[r])
    x_parts = [part(x, xs, c, norm_half(c)) for c in range(2)]
    g_parts = [part(g, gs, c) for c in range(2)]
    h2_parts = [part(h2_own, h2, c) for c in range(2)]
    hidden_own = vgu.shape[3] // 2
    hidden_block = hidden_own // rows

    def qkv_parts(t):
        for n, source in enumerate((wquery, wkey, wvalue)):
            target = vqkv.at[p.r, p.s, :, pl.ds(n * own_width, own_width)]
            yield columns(source, t, own_width), target

    def gu_parts(t):
        for n, source in enumerate((wgate, wup)):
            for r in range(rows):
                target = vgu.at[p.r, p.s, :, pl.ds(n * hidden_own + r * hidden_block, hidden_block)]
                yield columns(source, r * seqs + t, hidden_block), target

    qkv_swap = PartExchange(p, pool, qkv_parts, lambda b: vqkv.at[p.r, b], qkv_rows.forward)
    gu_swap = PartExchange(p, pool, gu_parts, lambda b: vgu.at[p.r, b], gu_rows.forward)
    out = SeqGather(p, pool, wout, lambda b: vout.at[p.r, b], out_rows.forward)
    gain = SeqExchange(p, pool, lambda t: gains, lambda b: vgains.at[p.r, b])
    heads_swap = SeqExchange(
        p, pool, lambda t: heads.at[rows_at(t, tokens), :], lambda b: columns(attended, b, own_width)
    )
    down_own = pool.take(1)

    gain.start()
    for member in x_parts:
        member.start()
    qkv_swap.start()
    out.start()
    for step in range(1, seqs):
        gain.step(step)
    gain.finish()
    gain_rows.forward(0)
    qkv_swap.settle_own()
    qkv_rows.forward(p.s)
    out_rows.forward(p.s, wout)
    pltpu.make_async_copy(wdown, vdown.at[p.r], down_own(0)).start()
    for block in range(down_blocks):
        down_fwd.forward(block, wdown.at[block])
    gain_rows.relay(0)
    gain_rows.finish()
    for pair in range(rows * seqs // 2):
        tile = vgains[2 * pair // seqs, 2 * pair % seqs] + vgains[2 * pair // seqs, 2 * pair % seqs + 1]
        gain_rows_out[:, pl.ds(pair * 2 * deep, 2 * deep)] = tile

    for c, member in enumerate(x_parts):
        member.settle_own()
        norm_half(c)(p.s)
    for k in range(1, p.n_hi):
        for member in x_parts:
            member.step(k)
        for step in (2 * k - 1, 2 * k):
            qkv_swap.step(step)
        out.step(k)
    gu_swap.start()
    qkv_swap.step(seqs - 1)
    gu_swap.settle_own()
    gu_rows.forward(p.s)
    for k in range(p.n_hi):
        for member in x_parts:
            member.aside(k)
        out.aside(k)
    for block in range(seqs):
        qkv_rows.relay(block)
    qkv_swap.finish()
    qkv_rows.finish()
    for member in g_parts:
        member.start()

    weights = vqkv.reshape(width, 3 * own_width)

    @pl.loop(0, seqs // 2)
    def _(step):
        tall = rows_at(step, 2 * tokens)
        qkv[tall, :] = nn(hn[tall, :], weights[...]).astype(jnp.bfloat16)

    own_heads = own_width // head_size
    share = -(-seqs // own_heads)
    for head in range(own_heads):
        attention(qkv, heads, key_place, query_low, query_high, shift, turned, head, head_size)
        for block in range(seqs)[head * share : (head + 1) * share]:
            out_rows.relay(block)
    heads_swap.start()
    out.finish()
    out_rows.finish()
    for r in range(rows):
        pltpu.make_async_copy(vout.at[r], out_held.at[r], copies.at[r]).start()
    for step in range(1, seqs):
        heads_swap.step(step)
    heads_swap.finish()
    for r in range(rows):
        settle(out_held.at[r], copies.at[r])
    out_weights = out_held.reshape(width, width)

    @pl.loop(0, width // 512)
    def _(c):
        lanes = rows_at(c, 512)
        middle[:, lanes] = xs[p.s, :, lanes].astype(jnp.float32) + nn(attended[...], out_weights[:, lanes])

    norm_rows(middle, h2_own, gain_rows_out.at[4:5, :])
    for member in h2_parts:
        member.start()
    for step in range(1, seqs):
        gu_swap.step(step)
    for k in range(1, p.n_hi):
        for member in g_parts + h2_parts:
            member.step(k)
    for block in range(down_blocks):
        down_fwd.relay(block)
    for block in range(seqs):
        gu_rows.relay(block)
    for k in range(p.n_hi):
        for member in g_parts + h2_parts:
            member.aside(k)
    for member in x_parts + g_parts + h2_parts + [gu_swap, down_fwd, gu_rows]:
        member.finish()
    settle(vdown.at[p.r], down_own(0))


def forward(rows, seqs, head_size, x, g, qkv_weights, gu_weights, wdown, wout, gains, meta):
    low, f32 = jnp.bfloat16, jnp.float32
    tokens, width = x.shape
    wdown = wdown.reshape(4, wdown.shape[0] // 4, width)
    own_width = width // seqs
    row_tokens = tokens * seqs
    deep = wout.shape[0]
    hidden_own = gu_weights[0].shape[1] // seqs
    shapes = (
        shape_of((seqs, tokens, width)),
        shape_of((rows, seqs, deep, 2 * hidden_own)),
        shape_of((rows,) + wdown.shape),
        shape_of((rows, seqs) + wout.shape),
        shape_of((seqs, tokens, width)),
        shape_of((rows, seqs, deep, 3 * own_width)),
        shape_of((row_tokens, width)),
        shape_of((row_tokens, 3 * own_width)),
        shape_of((tokens, width)),
        shape_of((tokens, width), f32),
        shape_of((8, width), f32),
    )
    scratch = [
        pltpu.VMEM((seqs, tokens, width), low),
        pltpu.VMEM((rows, seqs) + gains.shape, f32),
        pltpu.VMEM((row_tokens, own_width), low),
        pltpu.VMEM((head_size, row_tokens), f32),
        pltpu.VMEM((rows, seqs) + wout.shape, low),
        pltpu.VMEM((tokens, width), low),
        pltpu.SemaphoreType.DMA((rows,)),
    ]
    return call(
        functools.partial(forward_kernel, rows, seqs, head_size),
        shapes,
        1,
        (x, g) + qkv_weights + gu_weights + (wdown, wout, gains) + meta,
        [pl.ANY] * 10 + [pltpu.VMEM] * 4,
        (pl.ANY,) * 5 + (pltpu.VMEM,) * 6,
        scratch,
        800,
    )


def seq_reducers(place, pool, source, side, chain, target):
    half = target.shape[0] // 2
    members = []
    for c in range(2):
        piece = pl.ds(c * half, half)
        members.append(
            SeqReduce(
                place,
                pool,
                lambda b, piece=piece: source.at[b, piece],
                lambda b, piece=piece: side.at[b, piece],
                lambda slot, piece=piece: chain.at[slot, piece],
                target.at[piece],
            )
        )
    return members


def row_reducer(place, pool, source, core_slots, y_slots, target, add=add_into):
    return RowReduce(
        place,
        pool,
        source.shape[1],
        lambda r, b: source.at[r, b],
        lambda w, b: core_slots.at[w, b],
        lambda b: y_slots.at[b],
        lambda b: target.at[b],
        add,
    )


def ffn_kernel(
    rows,
    seqs,
    h2_in,
    gu_in,
    down_in,
    g_in,
    h2_sum,
    out_sum,
    gu_sum,
    down_sum,
    h2,
    gu_weights,
    down_weights,
    g,
    hidden,
    gu_grad,
    h2_part,
    h2_side,
    h2_chain,
    out_part,
    out_side,
    out_chain,
    gu_core,
    down_core,
    loads,
    sems,
):
    p, pool = Place(rows, seqs), Sems(sems)
    pairs = ((h2_in, h2), (gu_in, gu_weights), (g_in, g), (down_in, down_weights))
    for number, (source, target) in enumerate(pairs):
        pltpu.make_async_copy(source, target, loads.at[number]).start()
    greet(p.chain() + p.rows())
    tokens, width = h2_sum.shape
    hidden_own = hidden.shape[1]
    low = jnp.bfloat16
    h2_parts = seq_reducers(p, pool, h2_part, h2_side, h2_chain, h2_sum)
    out_parts = seq_reducers(p, pool, out_part, out_side, out_chain, out_sum)
    deep, down_deep = gu_sum.shape[1], down_sum.shape[1]

    def gu_at(r, b):
        return gu_weights.at[pl.ds(pl.multiple_of((r * seqs + b) * deep, deep), deep), :]

    def down_at(r, b):
        return down_weights.at[pl.ds(pl.multiple_of((r * down_sum.shape[0] + b) * down_deep, down_deep), down_deep), :]

    gu_rows = RowReduce(
        p, pool, seqs, gu_at, lambda w, b: gu_core.at[w, b], lambda b: gu_sum.at[b], lambda b: gu_sum.at[b]
    )
    down_rows = RowReduce(
        p,
        pool,
        down_sum.shape[0],
        down_at,
        lambda w, b: down_core.at[w, b],
        lambda b: down_sum.at[b],
        lambda b: down_sum.at[b],
    )
    for number, (source, target) in enumerate(pairs):
        settle(target, loads.at[number])

    def products(t):
        tall = rows_at(h2_parts[0].turn(t), 2 * tokens)

        @pl.loop(0, hidden_own // 256)
        def _(c):
            lanes, up_lanes = rows_at(c, 256), pl.ds(pl.multiple_of(hidden_own + c * 256, 256), 256)
            gate, up = nn(h2[tall, :], gu_weights[:, lanes]), nn(h2[tall, :], gu_weights[:, up_lanes])
            grad = nt(g[tall, :], down_weights[lanes, :])
            sig = jax.nn.sigmoid(gate)
            silu = gate * sig
            hidden[tall, lanes] = (silu * up).astype(low)
            gu_grad[tall, lanes] = (grad * up * (sig + silu * (1.0 - sig))).astype(low)
            gu_grad[tall, up_lanes] = (grad * silu).astype(low)

    def send_out(t):
        pair = h2_parts[0].turn(t)
        tall = rows_at(pair, 2 * tokens)

        @pl.loop(0, width // 512)
        def _(c):
            lanes = rows_at(c, 512)
            part = nn(hidden[tall, :], down_weights[:, lanes]).astype(low)
            out_part[2 * pair, :, lanes] = part[:tokens]
            out_part[2 * pair + 1, :, lanes] = part[tokens:]

        for member in out_parts:
            member.start(t)

    def send_h2(t):
        pair = h2_parts[0].turn(t)
        tall = rows_at(pair, 2 * tokens)

        @pl.loop(0, width // 512)
        def _(c):
            lanes = rows_at(c, 512)
            part = nt(gu_grad[tall, :], gu_weights[lanes, :]).astype(low)
            h2_part[2 * pair, :, lanes] = part[:tokens]
            h2_part[2 * pair + 1, :, lanes] = part[tokens:]

        for member in h2_parts:
            member.start(t)

    def sums(t, parts=None):
        for member in out_parts + h2_parts if parts is None else parts:
            member.step(t)

    def down_quarter(r):
        lanes = rows_at(r, hidden_own // rows)
        down_weights[lanes, :] = tn(hidden[:, lanes], g[...]).astype(low)

    def gu_quarter(r):
        @pl.loop(0, 2)
        def _(c):
            lanes = rows_at(2 * r + c, width // (2 * rows))
            gu_weights[lanes, :] = tn(h2[:, lanes], gu_grad[...]).astype(low)

    down_blocks, gu_blocks = range(down_sum.shape[0]), range(seqs)
    early = p.n_hi // 2
    for t in range(p.n_hi):
        products(t)
        send_out(t)
        if t < early:
            send_h2(t)
    sums(0, out_parts)
    down_quarter(p.r_far)
    for b in down_blocks:
        down_rows.start_far(b)
    down_quarter(p.r_core)
    for b in down_blocks:
        down_rows.start_core(b)
    down_quarter(p.r_y)
    for b in down_blocks:
        down_rows.step(b)
    for t in range(early, p.n_hi):
        send_h2(t)
    sums(0, h2_parts)
    gu_quarter(p.r_far)
    for b in gu_blocks:
        gu_rows.start_far(b)
    gu_quarter(p.r_y)
    for b in gu_blocks:
        gu_rows.step(b)
    gu_quarter(p.r_core)
    for b in gu_blocks:
        gu_rows.start_core(b)
    if p.n_hi > 2:
        sums(1)
    down_quarter(p.r)
    gu_quarter(p.r)
    for t in range(2 if p.n_hi > 2 else 1, p.n_hi):
        sums(t)
    for b in down_blocks:
        down_rows.close(b)
    for b in gu_blocks:
        gu_rows.close(b)
    for member in h2_parts + out_parts + [gu_rows, down_rows]:
        member.finish()


def slots(array, copies=()):
    return pltpu.VMEM(copies + array.shape[1:], array.dtype)


def seq_slots(array):
    half = array.shape[0] // 2
    return [
        pltpu.VMEM((half,) + array.shape[1:], array.dtype),
        pltpu.VMEM((half + 1,) + array.shape[1:], array.dtype),
    ]


def row_slots(array):
    return [slots(array, (2,)), slots(array)]


def row_blocks(rows, array, count):
    return array.reshape(rows, count, array.shape[0] // (rows * count), array.shape[1])


def ffn(rows, seqs, h2, wgu, wdown, g):
    low, f32 = jnp.bfloat16, jnp.float32
    row_tokens, width = h2.shape
    tokens, hidden_own = row_tokens // seqs, wdown.shape[0]
    gu_dims, down_dims = (seqs, width // (rows * seqs), 2 * hidden_own), (4, hidden_own // (4 * rows), width)
    part = shape_of((seqs, tokens, width))
    shapes = (shape_of((tokens, width), f32), shape_of((tokens, width), f32), shape_of(gu_dims), shape_of(down_dims))
    scratch = (
        [pltpu.VMEM(array.shape, low) for array in (h2, wgu, wdown, g)]
        + [pltpu.VMEM((row_tokens, hidden_own), low), pltpu.VMEM((row_tokens, 2 * hidden_own), low)]
        + [pltpu.VMEM(part.shape, low)]
        + seq_slots(part)
        + [pltpu.VMEM(part.shape, low)]
        + seq_slots(part)
        + [pltpu.VMEM((2,) + gu_dims, low), pltpu.VMEM((2,) + down_dims, low)]
        + [pltpu.SemaphoreType.DMA((4,))]
    )
    return call(
        functools.partial(ffn_kernel, rows, seqs),
        shapes,
        4,
        (h2, wgu, wdown, g),
        [pl.ANY] * 4,
        (pltpu.VMEM,) * 4,
        scratch,
        320,
    )


class ColumnExchange:
    def __init__(self, place, sems, piece, parts):
        self.p, self.piece, self.parts = place, piece, parts
        n = place.seq_count
        self.own, self.send, self.recv = sems.take(1), sems.take(n), sems.take(n)

    def start(self):
        p, s = self.p, self.p.s
        for step in range(p.seq_count):
            t = p.peer(step)
            piece = self.piece(t)
            for offset, width, target in self.parts(s):
                source = piece.at[:, pl.ds(offset, width)]
                if step == 0:
                    pltpu.make_async_copy(source, target, self.own(0)).start()
                else:
                    push(source, target, self.send(step), self.recv(s), (p.r, t))

    def finish(self):
        p = self.p
        settle(self.piece(p.s), self.own(0))
        for step in range(1, p.seq_count):
            settle(self.piece(p.s), self.send(step))
            settle(self.piece(p.s), self.recv(p.peer(step)))


def attention_back(qkv, do, dqkv, key_place, query_low, query_high, shift, dq_turned, head_size):
    tokens, own_width = do.shape
    scale = head_size ** (-0.5)
    keys_step = 256
    for head in range(own_width // head_size):
        lanes = pl.ds(head * head_size, head_size)
        key_lanes = pl.ds(own_width + head * head_size, head_size)
        value_lanes = pl.ds(2 * own_width + head * head_size, head_size)
        dq_turned[...] = jnp.zeros_like(dq_turned)

        @pl.loop(0, tokens // keys_step)
        def _(step):
            rows = pl.ds(pl.multiple_of(step * keys_step, keys_step), keys_step)
            key, value = qkv[rows, key_lanes], qkv[rows, value_lanes]
            queries, grads = qkv[:, lanes], do[:, lanes]
            places = key_place[rows, :]
            allowed = (places >= query_low[...]) & (places <= query_high[...])
            scores = nt(key, queries) * scale - shift[...]
            sig = jnp.where(allowed, jax.nn.sigmoid(scores), 0.0)
            score_grad = (nt(value, grads) * sig * (1.0 - sig)).astype(jnp.bfloat16)
            dqkv[rows, value_lanes] = nn(sig.astype(jnp.bfloat16), grads).astype(jnp.bfloat16)
            dqkv[rows, key_lanes] = (nn(score_grad, queries) * scale).astype(jnp.bfloat16)
            dq_turned[...] += nn(key.T, score_grad)

        dqkv[:, lanes] = (dq_turned[...].T * scale).astype(jnp.bfloat16)


def back_kernel(
    rows,
    seqs,
    head_size,
    do_own,
    qkv_in,
    hn_in,
    wqkv_in,
    out_in,
    gu,
    gain_two_part,
    gain_one,
    key_place,
    query_low,
    query_high,
    shift,
    hn_sum,
    out_sum,
    query_got,
    key_got,
    value_got,
    gate_got,
    up_got,
    gain_got,
    do,
    dqkv,
    dq_turned,
    hn_part,
    hn_side,
    hn_chain,
    grad_qkv,
    qkv_core,
    qkv_y,
    out_core,
    out_y,
    out_side,
    out_chain,
    gains,
    gain_core,
    gain_y,
    qkv,
    hn,
    wqkv,
    out_own,
    loads,
    sems,
):
    p, pool = Place(rows, seqs), Sems(sems)
    pairs = (
        (qkv_in, qkv),
        (out_in.at[p.r_y], out_own.at[0]),
        (wqkv_in, wqkv),
        (hn_in, hn),
        (out_in.at[p.r], out_own.at[1]),
    )
    for number, (source, target) in enumerate(pairs):
        pltpu.make_async_copy(source, target, loads.at[number]).start()
    greet(p.peers() + p.rows())
    tokens, own_width = do.shape
    block_tokens = tokens // seqs
    width = wqkv.shape[0]

    def block_rows(b):
        return pl.ds(pl.multiple_of(b * block_tokens, block_tokens), block_tokens)

    do_swap = SeqExchange(
        p, pool, lambda t: columns(do_own, t, own_width), lambda b: do.at[block_rows(b), :]
    )
    do_swap.start()
    out_rows = RowReduce(
        p,
        pool,
        seqs,
        lambda r, b: out_in.at[r, b],
        lambda w, b: out_core.at[w, b],
        lambda b: out_y.at[b],
        lambda b: out_y.at[b],
        own=lambda w, b: out_own.at[w, b],
    )
    for b in range(seqs):
        out_rows.start(b)
    hidden_own = gu.shape[2] // 2
    block = hidden_own // rows

    def gu_parts(s):
        for n, target in ((0, gate_got), (1, up_got)):
            for r in range(rows):
                yield n * hidden_own + r * block, block, columns(target, r * seqs + s, block)

    gu_swap = ColumnExchange(p, pool, lambda t: gu.at[t], gu_parts)

    def qkv_parts(s):
        for n, target in enumerate((query_got, key_got, value_got)):
            yield n * own_width, own_width, columns(target, s, own_width)

    qkv_swap = ColumnExchange(p, pool, lambda t: qkv_y.at[t], qkv_parts)
    qkv_rows = row_reducer(p, pool, grad_qkv, qkv_core, qkv_y, qkv_y)
    hn_parts = seq_reducers(p, pool, hn_part, hn_side, hn_chain, hn_sum)
    out_seq = SeqReduce(
        p, pool, lambda b: out_y.at[b], lambda b: out_side.at[b], lambda slot: out_chain.at[slot], out_sum
    )
    quarter = width // rows
    gain_rows = RowReduce(
        p,
        pool,
        1,
        lambda r, b: columns(gains, r, quarter),
        lambda w, b: gain_core.at[w],
        lambda b: gain_y,
        lambda b: gain_y,
        add_small,
    )
    gain_width = 2 * quarter // seqs
    gain_swap = SeqExchange(
        p, pool, lambda t: columns(gain_y, t // 2, gain_width), lambda b: gain_got.at[b]
    )

    for step in range(1, seqs):
        do_swap.step(step)
    settle(do.at[block_rows(p.s), :], do_swap.own(0))
    gu_swap.start()
    settle(out_own.at[0], loads.at[1])
    for b in range(seqs):
        out_rows.step(b)
    settle(qkv, loads.at[0])
    attention_back(qkv, do, dqkv, key_place, query_low, query_high, shift, dq_turned, head_size)

    for number in (2, 3, 4):
        settle(pairs[number][1], loads.at[number])
    gains[0:8, :] = jnp.zeros_like(gains[0:8, :])
    gains[8:16, :] = gain_two_part[...]
    column_step = 512
    for t in range(p.n_hi):
        pair = hn_parts[0].turn(t)
        tall = pl.ds(pl.multiple_of(pair * 2 * block_tokens, 2 * block_tokens), 2 * block_tokens)

        @pl.loop(0, width // column_step)
        def _(c):
            lanes = pl.ds(pl.multiple_of(c * column_step, column_step), column_step)
            part = nt(dqkv[tall, :], wqkv[lanes, :])
            hn_part[2 * pair, :, lanes] = part[:block_tokens].astype(jnp.bfloat16)
            hn_part[2 * pair + 1, :, lanes] = part[block_tokens:].astype(jnp.bfloat16)
            terms = part * hn[tall, lanes].astype(jnp.float32)
            gains[0:8, lanes] += jnp.sum(terms.reshape(-1, 8, column_step), axis=0)

        for member in hn_parts:
            member.start(t)
    gains[0:8, :] = gains[0:8, :] / gain_one[...]
    gain_rows.start(0)

    @pl.loop(0, width // 256)
    def _(c):
        lanes = pl.ds(pl.multiple_of(c * 256, 256), 256)
        total = tn(hn[:, lanes], dqkv[...]).astype(jnp.bfloat16)
        piece = total.reshape((4,) + (total.shape[0] // 4, total.shape[1]))
        for n in range(4):
            grad_qkv[c * 4 // seqs, lax.rem(c * 4, seqs) + n] = piece[n]

    for b in range(seqs):
        qkv_rows.start(b)
    gain_rows.step(0)
    for t in range(p.n_hi):
        for member in hn_parts:
            member.step(t)
        if t == 0:
            for b in range(seqs):
                qkv_rows.step(b)
            gain_rows.close(0)
            gain_swap.start()
        if t == p.n_hi // 2 - 1:
            for b in range(seqs):
                out_rows.close(b)
            for k in range(p.n_hi):
                out_seq.start(k)
        if t == p.n_hi - 2:
            for b in range(seqs):
                qkv_rows.close(b)
            qkv_swap.start()
    for t in range(p.n_hi):
        out_seq.step(t)
    for step in range(1, seqs):
        gain_swap.step(step)
        settle(do.at[block_rows(p.s), :], do_swap.send(step))
    for member in hn_parts + [out_rows, qkv_rows, gain_rows, gu_swap, qkv_swap, out_seq, gain_swap]:
        member.finish()


def back(rows, seqs, head_size, do_own, qkv, hn, wqkv, out, gu, gain_two_part, gain_one, meta):
    tokens, own_width = qkv.shape[0], qkv.shape[1] // 3
    width = hn.shape[1]
    low = jnp.bfloat16
    out = row_blocks(rows, out, seqs)
    block_tokens = tokens // seqs
    hn_dims, qkv_dims = (seqs, block_tokens, width), (rows, seqs, width // (rows * seqs), 3 * own_width)
    deep = width // (rows * seqs)
    quarter = width // rows
    got = shape_of((deep, width))
    gu_got = shape_of((deep, gu.shape[2] // 2 * seqs))
    gain_width = 2 * quarter // seqs
    shapes = (
        shape_of(hn_dims[1:], jnp.float32),
        shape_of(out.shape[2:]),
        got,
        got,
        got,
        gu_got,
        gu_got,
        shape_of((seqs, 16, gain_width), jnp.float32),
    )
    hn_like, qkv_like, out_like = shape_of(hn_dims), shape_of(qkv_dims), shape_of(out.shape)
    scratch = (
        [
            pltpu.VMEM((tokens, own_width), low),
            pltpu.VMEM(qkv.shape, low),
            pltpu.VMEM((head_size, tokens), jnp.float32),
            pltpu.VMEM(hn_dims, low),
        ]
        + seq_slots(hn_like)
        + [pltpu.VMEM(qkv_dims, low)]
        + row_slots(qkv_like)
        + row_slots(out_like)
        + seq_slots(shape_of(out.shape[1:]))
        + [
            pltpu.VMEM((16, width), jnp.float32),
            pltpu.VMEM((2, 16, quarter), jnp.float32),
            pltpu.VMEM((16, quarter), jnp.float32),
            pltpu.VMEM(qkv.shape, low),
            pltpu.VMEM(hn.shape, low),
            pltpu.VMEM(wqkv.shape, low),
            pltpu.VMEM((2,) + out.shape[1:], low),
            pltpu.SemaphoreType.DMA((5,)),
        ]
    )
    return call(
        functools.partial(back_kernel, rows, seqs, head_size),
        shapes,
        6,
        (do_own, qkv, hn, wqkv, out, gu, gain_two_part, gain_one) + meta,
        [pltpu.VMEM] + [pl.ANY] * 4 + [pltpu.VMEM] * 7,
        (pltpu.VMEM,) * 5 + (pl.ANY,) * 2 + (pltpu.VMEM,),
        scratch,
        480,
    )


def dot(left, right, left_axis=1, right_axis=0):
    return lax.dot_general(
        left, right, (((left_axis,), (right_axis,)), ((), ())), preferred_element_type=jnp.float32
    )


def split_local(
    rows,
    seqs,
    inputs,
    lengths,
    w_query,
    w_key,
    w_value,
    w_out,
    gain_attn,
    w_gate,
    w_up,
    w_down,
    gain_mlp,
    cotangent,
):
    low, f32 = jnp.bfloat16, jnp.float32
    tokens, width = inputs.shape[1], inputs.shape[2]
    deep = w_query.shape[0]
    row_tokens = tokens * seqs
    head_size = width // HEADS
    own_width = width // seqs
    hidden_own = w_gate.shape[1] // seqs

    side = lax.rem(lax.axis_index("seq"), 2)
    lane = lax.broadcasted_iota(jnp.int32, (8, 2 * deep), 1)
    both = [jnp.concatenate([gain, gain]).astype(f32)[None, :] for gain in (gain_attn, gain_mlp)]
    number = lax.broadcasted_iota(jnp.int32, (8, 2 * deep), 0)
    gains_own = jnp.where(lane // deep == side, jnp.where(number < 4, both[0], both[1]), 0.0)
    x_low, g_low = inputs[0], cotangent[0]

    def places(shape, axis):
        index = lax.broadcasted_iota(jnp.int32, shape, axis)
        block, within = index // tokens, lax.rem(index, tokens)
        segment = position = length_of = jnp.zeros_like(index)
        begin = 0
        for n in range(lengths.shape[1]):
            unit = lengths[0, n] // (2 * seqs)
            inside = (within >= begin) & (within < begin + 2 * unit)
            local = within - begin
            here = jnp.where(local < unit, block * unit + local, (2 * seqs - 1 - block) * unit + local - unit)
            segment = jnp.where(inside, n, segment)
            position = jnp.where(inside, here, position)
            length_of = jnp.where(inside, lengths[0, n], length_of)
            begin = begin + 2 * unit
        return segment * row_tokens, segment * row_tokens + position, length_of

    query_low, query_high, length_of = places((1, row_tokens), 1)
    meta = (places((row_tokens, 1), 0)[1], query_low, query_high, jnp.log(length_of.astype(f32)))
    g_all, wgu, wdown, wout, h2, wqkv, hn, qkv, attended, middle, gains = forward(
        rows,
        seqs,
        head_size,
        x_low,
        g_low,
        (w_query, w_key, w_value),
        (w_gate, w_up),
        w_down,
        w_out,
        gains_own,
        meta,
    )
    gain_one, gain_two = gains[0:1], gains[4:5]
    wqkv = wqkv.reshape(width, 3 * own_width)
    wgu = wgu.reshape(width, 2 * hidden_own)
    wdown = wdown.reshape(hidden_own, width)
    wout = wout.reshape(width, width)
    g_all = g_all.reshape(row_tokens, width)
    h2 = h2.reshape(row_tokens, width)
    residual = x_low.astype(f32)
    h2_grad, out_sum, sum_gu, sum_down = ffn(rows, seqs, h2, wgu, wdown, g_all)
    output = (middle + out_sum).astype(low)

    inverse = lax.rsqrt(jnp.mean(middle * middle, axis=-1, keepdims=True) + EPSILON)
    scaled_grad = gain_two * h2_grad
    gain_two_part = jnp.sum((h2_grad * middle * inverse).reshape(-1, 8, width), axis=0)
    middle_grad = (
        g_low.astype(f32)
        + inverse * scaled_grad
        - middle * inverse**3 * jnp.mean(scaled_grad * middle, axis=-1, keepdims=True)
    )
    branch = middle_grad.astype(low)
    grad_out = dot(attended, branch, 0, 0).astype(low)
    do_own = dot(branch, wout, 1, 1).astype(low)
    hn_grad, sum_out, got_query, got_key, got_value, got_gate, got_up, got_gain = back(
        rows, seqs, head_size, do_own, qkv, hn, wqkv, grad_out, sum_gu, gain_two_part, gain_one, meta
    )
    spread_inverse = lax.rsqrt(jnp.mean(residual * residual, axis=-1, keepdims=True) + EPSILON)
    scaled_grad = gain_one * hn_grad
    input_grad = (
        middle_grad
        + spread_inverse * scaled_grad
        - residual * spread_inverse**3 * jnp.mean(scaled_grad * residual, axis=-1, keepdims=True)
    )
    gain_sums = jnp.sum(got_gain, axis=0).reshape(2, 8, 2, deep).sum(axis=1)
    gain_sums = lax.dynamic_index_in_dim(gain_sums, lax.rem(lax.axis_index("seq"), 2), 1, keepdims=False)
    return (
        output[None],
        input_grad[None],
        got_query.astype(f32),
        got_key.astype(f32),
        got_value.astype(f32),
        sum_out.astype(f32),
        gain_sums[0],
        got_gate.astype(f32),
        got_up.astype(f32),
        sum_down.reshape(w_down.shape).astype(f32),
        gain_sums[1],
    )


def solution(mesh):
    placed = (
        P("row", "seq", None),
        P("row", None),
        P(("row", "seq"), None),
        P(("row", "seq"), None),
        P(("row", "seq"), None),
        P(("row", "seq"), None),
        P(("row", "seq")),
        P(("row", "seq"), None),
        P(("row", "seq"), None),
        P(("row", "seq"), None),
        P(("row", "seq")),
        P("row", "seq", None),
    )
    row_count, seq_count = mesh.shape["row"], mesh.shape["seq"]
    if row_count == 4 and seq_count % 2 == 0 and HEADS % seq_count == 0:
        local = functools.partial(split_local, row_count, seq_count)
    else:
        local = gathered_local
    return jax.shard_map(
        local,
        mesh=mesh,
        in_specs=placed,
        out_specs=(
            P("row", "seq", None),
            P("row", "seq", None),
            P(("row", "seq"), None),
            P(("row", "seq"), None),
            P(("row", "seq"), None),
            P(("row", "seq"), None),
            P(("row", "seq")),
            P(("row", "seq"), None),
            P(("row", "seq"), None),
            P(("row", "seq"), None),
            P(("row", "seq")),
        ),
        check_vma=False,
    )
```

profile of v0, /device:TPU:0, one launch (start us, length us, event | category | flops | bytes accessed | tf_op | source)
XLA Modules:
  0.0 546.1 jit_solution(7505632848834652935)
XLA Ops:
  0.6 1.3 fusion.38
  7.2 1.3 fusion.15.key_place
  8.5 0.6 fusion.35
  9.1 1.9 convert_log_fusion.shift
  11.0 0.8 maximum_convert_fusion
  11.9 0.7 select_select_fusion.gains
  12.5 232.8 %shard_map.203 = (bf16[8,128,2048]{2,1,0:T(8,128)(2,1)}, bf16[4,8,64,2048]{3,2,1,0:T(8,128)(2,1)}, bf16[4,4,64,2048]{3,2,1,0:T(8,128)(2,1)}, bf16[4,8,64,2048]{3...) custom-call(bf16[128,2048]{1,0:T(8,128)(2,1)} %bitcast.38, ...), custom_call_target="tpu_custom_call" | custom-call | tf_op jit(solution)/shard_map/pallas_call | solution.py:717
  245.4 117.5 %shard_map.204 = (f32[128,2048]{1,0:T(8,128)}, f32[128,2048]{1,0:T(8,128)}, bf16[8,64,2048]{2,1,0:T(8,128)(2,1)}, bf16[4,64,2048]{2,1,0:T(8,128)(2,1)}) custom-call(bf16[1024,2048]{1,0:T(8,128)(2,1)} %bitcast.41, bf16[2048,2048]{1,0:T(8,128)(2,1)} %bitcast.37, bf16[1024,2048]{1,0:T(8,128)(2,1)} %bitcast.40, bf16[1024,2048]{1,0:T(8,128)(2,1)} %bitcast.39), custom_call_target="tpu_custom_call" | custom-call | tf_op jit(solution)/shard_map/pallas_call | solution.py:717
  362.9 1.6 fusion.37
  364.5 1.5 multiply_reduce_fusion.1
  366.0 2.1 bitcast_reduce_fusion.gain_two_part
  368.1 1.2 multiply_subtract_fusion
  369.3 5.6 %convolution_convert_fusion = bf16[2048,2048]{1,0:T(8,128)(2,1)} fusion(bf16[128,2048]{1,0:T(8,128)(2,1)S(1)} %copy-done.6, f32[128,2048]{1,0:T(8,128)S(1)} %get-tuple-element.61), kind=kOutput, calls=%fused_computation | convolution fusion | flops 1078198272 | bytes 9961472 | tf_op jit(solution)/shard_map/dot_general | solution.py:1542
  375.0 3.7 convolution_convert_fusion.1.do_own
  378.7 154.1 %shard_map.205 = (f32[128,2048]{1,0:T(8,128)}, bf16[64,2048]{1,0:T(8,128)(2,1)}, bf16[64,2048]{1,0:T(8,128)(2,1)}, bf16[64,2048]{1,0:T(8,128)(2,1)}, bf16[64,204...) custom-call(bf16[128,2048]{1,0:T(8,128)(2,1)} %convolution_convert_fusion.1.do_own, ...), custom_call_target="tpu_custom_call" | custom-call | tf_op jit(solution)/shard_map/pallas_call | solution.py:717
  532.8 2.8 convert_element_type.80
  535.6 2.7 convert_element_type.81
  538.7 1.3 fusion.3
  540.0 0.8 convert_element_type.76
  540.8 0.8 convert_element_type.77
  541.7 0.8 convert_element_type.78
  542.5 0.8 convert_element_type.79
  543.5 0.5 dynamic-slice_bitcast_fusion
  544.0 1.6 bitcast_convert_fusion
  (46 shorter events, 0.5 us)
Async XLA Ops:
  245.4 119.2 %copy-start = (f32[128,2048]{1,0:T(8,128)S(1)}, f32[128,2048]{1,0:T(8,128)}, u32[]{:S(2)}) copy-start(f32[128,2048]{1,0:T(8,128)} %get-tuple-element.34) | copy-start | bytes 3145732
  362.9 5.3 copy-start.1
  362.9 5.2 copy-start.2
  362.9 5.2 copy-start.5
  362.9 5.2 copy-start.8
  366.0 3.3 copy-start.6
  368.1 6.8 %slice-start = ((s8[8388608]{0:T(1024)(128)(4,1)}), s8[4194304]{0:T(1024)(128)(4,1)S(1)}, s32[]{:S(2)}) async-start(s8[8388608]{0:T(1024)(128)(4,1)} %bitcast.34), calls=%async_computation | async-start | bytes 8388608
  369.3 5.6 %slice-start.1 = ((s8[8388608]{0:T(1024)(128)(4,1)}), s8[4194304]{0:T(1024)(128)(4,1)S(1)}, s32[]{:S(2)}) async-start(s8[8388608]{0:T(1024)(128)(4,1)} %bitcast.34), calls=%async_computation.1 | async-start | bytes 8388608
  532.8 5.6 %copy-start.3 = (bf16[1,128,2048]{2,1,0:T(8,128)(2,1)S(1)}, bf16[1,128,2048]{2,1,0:T(8,128)(2,1)}, u32[]{:S(2)}) copy-start(bf16[1,128,2048]{2,1,0:T(8,128)(2,1)} %param.12) | copy-start | bytes 1572868
  532.8 5.6 %copy-start.4 = (f32[128,2048]{1,0:T(8,128)S(1)}, f32[128,2048]{1,0:T(8,128)}, u32[]{:S(2)}) copy-start(f32[128,2048]{1,0:T(8,128)} %get-tuple-element.48) | copy-start | bytes 3145732
  532.8 5.6 %copy-start.13 = (f32[1,2048]{1,0:T(1,128)S(1)}, f32[1,2048]{1,0:T(1,128)}, u32[]{:S(2)}) copy-start(f32[1,2048]{1,0:T(1,128)} %get-tuple-element.63.gain_one) | copy-start | bytes 24580
  535.6 4.4 copy-start.12
  535.6 5.3 copy-start.11
  538.3 3.3 copy-start.10
  538.3 4.2 copy-start.9
  538.3 5.0 copy-start.14
  538.4 5.6 %copy-start.7 = (bf16[4,64,2048]{2,1,0:T(8,128)(2,1)S(1)}, bf16[4,64,2048]{2,1,0:T(8,128)(2,1)}, u32[]{:S(2)}) copy-start(bf16[4,64,2048]{2,1,0:T(8,128)(2,1)} %get-tuple-element.56) | copy-start | bytes 3145732
where the time goes:
time: 553 us; the launch traced here: 546 us
  Pallas kernels  504 us (91%)
  other arithmetic  22.2 us (4%)
  matrix products  9.31 us (2%)
  between operations  6.55 us (1%)
    pallas_call x3, Pallas kernels, call(): pl.pallas_call(kernel, out_shape=shapes, in_specs=[pl.BlockSpec(memory_sp...  504 us

commit v1 on v0

--- a/solution.py
+++ b/solution.py
@@ -384,9 +384,24 @@
     return None
 
 
+class Stores:
+    def __init__(self, sems):
+        self.sems, self.open = sems, []
+
+    def start(self, source, target):
+        sem = self.sems.take(1)(0)
+        pltpu.make_async_copy(source, target, sem).start()
+        self.open.append((target, sem))
+
+    def finish(self):
+        for target, sem in self.open:
+            settle(target, sem)
+
+
 class SeqGather:
-    def __init__(self, place, sems, source, at, arrived=no_op):
+    def __init__(self, place, sems, source, at, arrived=no_op, arrived_aside=None):
         self.p, self.source, self.at, self.arrived = place, source, at, arrived
+        self.arrived_aside = arrived_aside or arrived
         self.own_done = False
         n = place.n_hi
         self.own, self.up, self.down = sems.take(1), sems.take(n), sems.take(n)
@@ -438,20 +453,20 @@
         if k == 0:
             block = 2 * p.hi + 1 - p.lo
             settle(self.at(block), self.recv(block))
-            self.arrived(block)
+            self.arrived_aside(block)
             return
 
         @pl.when(p.hi >= k)
         def _():
             block = 2 * (p.hi - k) + 1 - p.lo
             settle(self.at(block), self.recv(block))
-            self.arrived(block)
+            self.arrived_aside(block)
 
         @pl.when(p.hi + k < p.n_hi)
         def _():
             block = 2 * (p.hi + k) + 1 - p.lo
             settle(self.at(block), self.recv(block))
-            self.arrived(block)
+            self.arrived_aside(block)
 
     def settle_own(self):
         settle(self.at(self.p.s), self.own(0))
@@ -752,6 +767,42 @@
         rows = rows_at(tile, 16)
         values = source[rows, :].astype(jnp.float32)
         target[rows, :] = rms_norm(values, gain[...]).astype(target.dtype)
+
+
+def places(lengths, shape, axis, tokens, seqs):
+    row_tokens = tokens * seqs
+    index = lax.broadcasted_iota(jnp.int32, shape, axis)
+    block, within = index // tokens, lax.rem(index, tokens)
+    segment = position = length_of = jnp.zeros_like(index)
+    begin = 0
+    for n in range(lengths.shape[1]):
+        length = lengths[0, n]
+        unit = length // (2 * seqs)
+        inside = (within >= begin) & (within < begin + 2 * unit)
+        local = within - begin
+        here = jnp.where(local < unit, block * unit + local, (2 * seqs - 1 - block) * unit + local - unit)
+        segment = jnp.where(inside, n, segment)
+        position = jnp.where(inside, here, position)
+        length_of = jnp.where(inside, length, length_of)
+        begin = begin + 2 * unit
+    return segment * row_tokens, segment * row_tokens + position, length_of
+
+
+def fill_meta(lengths, key_place, query_low, query_high, shift, tokens, seqs):
+    key_place[...] = places(lengths, key_place.shape, 0, tokens, seqs)[1]
+    low, high, length_of = places(lengths, query_low.shape, 1, tokens, seqs)
+    query_low[...] = low
+    query_high[...] = high
+    shift[...] = jnp.log(length_of.astype(jnp.float32))
+
+
+def meta_scratch(row_tokens):
+    return [
+        pltpu.VMEM((row_tokens, 1), jnp.int32),
+        pltpu.VMEM((1, row_tokens), jnp.int32),
+        pltpu.VMEM((1, row_tokens), jnp.int32),
+        pltpu.VMEM((1, row_tokens), jnp.float32),
+    ]
 
 
 def attention(qkv, attended, key_place, query_low, query_high, shift, turned, head, head_size):
@@ -789,27 +840,33 @@
     wdown,
     wout,
     gains,
-    key_place,
-    query_low,
-    query_high,
-    shift,
+    lengths,
     gs,
     vgu,
     vdown,
     vout,
     h2,
+    vqkv_kept,
+    hn_kept,
+    qkv_kept,
+    attended_kept,
+    middle_kept,
+    gain_rows_out,
     vqkv,
     hn,
     qkv,
     attended,
     middle,
-    gain_rows_out,
     xs,
     vgains,
     heads,
     turned,
     out_held,
     h2_own,
+    key_place,
+    query_low,
+    query_high,
+    shift,
     copies,
     sems,
 ):
@@ -821,14 +878,15 @@
     deep = wout.shape[0]
     down_blocks = vdown.shape[1]
 
-    def part(source, target, c, arrived=no_op):
+    def part(source, target, c, arrived_aside=None):
         piece = pl.ds(c * half, half)
-        return SeqGather(p, pool, source.at[piece], lambda b: target.at[b, piece], arrived)
+        return SeqGather(p, pool, source.at[piece], lambda b: target.at[b, piece], no_op, arrived_aside)
 
     def norm_half(c):
-        def run(b):
-            start = pl.multiple_of(b * tokens + c * half, half)
-            norm_rows(xs.at[b, pl.ds(c * half, half)], hn.at[pl.ds(start, half), :], gain_rows_out.at[0:1, :])
+        def run(block):
+            for b in (block, block + 1 - 2 * lax.rem(block, 2)):
+                start = pl.multiple_of(b * tokens + c * half, half)
+                norm_rows(xs.at[b, pl.ds(c * half, half)], hn.at[pl.ds(start, half), :], gain_rows_out.at[0:1, :])
 
         return run
 
@@ -861,7 +919,7 @@
     heads_swap = SeqExchange(
         p, pool, lambda t: heads.at[rows_at(t, tokens), :], lambda b: columns(attended, b, own_width)
     )
-    down_own = pool.take(1)
+    stores = Stores(pool)
 
     gain.start()
     for member in x_parts:
@@ -875,7 +933,7 @@
     qkv_swap.settle_own()
     qkv_rows.forward(p.s)
     out_rows.forward(p.s, wout)
-    pltpu.make_async_copy(wdown, vdown.at[p.r], down_own(0)).start()
+    stores.start(wdown, vdown.at[p.r])
     for block in range(down_blocks):
         down_fwd.forward(block, wdown.at[block])
     gain_rows.relay(0)
@@ -884,29 +942,32 @@
         tile = vgains[2 * pair // seqs, 2 * pair % seqs] + vgains[2 * pair // seqs, 2 * pair % seqs + 1]
         gain_rows_out[:, pl.ds(pair * 2 * deep, 2 * deep)] = tile
 
-    for c, member in enumerate(x_parts):
+    fill_meta(lengths, key_place, query_low, query_high, shift, tokens, seqs)
+    for member in x_parts:
         member.settle_own()
-        norm_half(c)(p.s)
     for k in range(1, p.n_hi):
         for member in x_parts:
             member.step(k)
-        for step in (2 * k - 1, 2 * k):
-            qkv_swap.step(step)
+    for step in range(1, seqs):
+        qkv_swap.step(step)
+    for k in range(1, p.n_hi):
         out.step(k)
     gu_swap.start()
-    qkv_swap.step(seqs - 1)
     gu_swap.settle_own()
     gu_rows.forward(p.s)
     for k in range(p.n_hi):
         for member in x_parts:
             member.aside(k)
-        out.aside(k)
+    for member in g_parts:
+        member.start()
     for block in range(seqs):
         qkv_rows.relay(block)
+    for k in range(p.n_hi):
+        out.aside(k)
     qkv_swap.finish()
     qkv_rows.finish()
-    for member in g_parts:
-        member.start()
+    stores.start(hn, hn_kept)
+    stores.start(vqkv, vqkv_kept)
 
     weights = vqkv.reshape(width, 3 * own_width)
 
@@ -915,13 +976,15 @@
         tall = rows_at(step, 2 * tokens)
         qkv[tall, :] = nn(hn[tall, :], weights[...]).astype(jnp.bfloat16)
 
+    stores.start(qkv, qkv_kept)
     own_heads = own_width // head_size
-    share = -(-seqs // own_heads)
     for head in range(own_heads):
         attention(qkv, heads, key_place, query_low, query_high, shift, turned, head, head_size)
-        for block in range(seqs)[head * share : (head + 1) * share]:
-            out_rows.relay(block)
     heads_swap.start()
+    for block in range(seqs):
+        out_rows.relay(block)
+    for member in g_parts:
+        member.step(1)
     out.finish()
     out_rows.finish()
     for r in range(rows):
@@ -939,13 +1002,19 @@
         middle[:, lanes] = xs[p.s, :, lanes].astype(jnp.float32) + nn(attended[...], out_weights[:, lanes])
 
     norm_rows(middle, h2_own, gain_rows_out.at[4:5, :])
+    stores.start(attended, attended_kept)
+    stores.start(middle, middle_kept)
     for member in h2_parts:
         member.start()
     for step in range(1, seqs):
         gu_swap.step(step)
-    for k in range(1, p.n_hi):
-        for member in g_parts + h2_parts:
+    for k in range(2, p.n_hi):
+        for member in g_parts:
             member.step(k)
+        for member in h2_parts:
+            member.step(k - 1)
+    for member in h2_parts:
+        member.step(p.n_hi - 1)
     for block in range(down_blocks):
         down_fwd.relay(block)
     for block in range(seqs):
@@ -955,10 +1024,10 @@
             member.aside(k)
     for member in x_parts + g_parts + h2_parts + [gu_swap, down_fwd, gu_rows]:
         member.finish()
-    settle(vdown.at[p.r], down_own(0))
-
-
-def forward(rows, seqs, head_size, x, g, qkv_weights, gu_weights, wdown, wout, gains, meta):
+    stores.finish()
+
+
+def forward(rows, seqs, head_size, x, g, qkv_weights, gu_weights, wdown, wout, gains, lengths):
     low, f32 = jnp.bfloat16, jnp.float32
     tokens, width = x.shape
     wdown = wdown.reshape(4, wdown.shape[0] // 4, width)
@@ -979,22 +1048,23 @@
         shape_of((tokens, width), f32),
         shape_of((8, width), f32),
     )
-    scratch = [
+    scratch = [pltpu.VMEM(member.shape, member.dtype) for member in shapes[5:10]] + [
         pltpu.VMEM((seqs, tokens, width), low),
         pltpu.VMEM((rows, seqs) + gains.shape, f32),
         pltpu.VMEM((row_tokens, own_width), low),
         pltpu.VMEM((head_size, row_tokens), f32),
         pltpu.VMEM((rows, seqs) + wout.shape, low),
         pltpu.VMEM((tokens, width), low),
+        *meta_scratch(row_tokens),
         pltpu.SemaphoreType.DMA((rows,)),
     ]
     return call(
         functools.partial(forward_kernel, rows, seqs, head_size),
         shapes,
         1,
-        (x, g) + qkv_weights + gu_weights + (wdown, wout, gains) + meta,
-        [pl.ANY] * 10 + [pltpu.VMEM] * 4,
-        (pl.ANY,) * 5 + (pltpu.VMEM,) * 6,
+        (x, g) + qkv_weights + gu_weights + (wdown, wout, gains, lengths),
+        [pltpu.VMEM] * 10 + [pltpu.SMEM],
+        (pl.ANY,) * 10 + (pltpu.VMEM,),
         scratch,
         800,
     )
@@ -1038,6 +1108,10 @@
     gu_in,
     down_in,
     g_in,
+    h2_kept,
+    out_kept,
+    gu_kept,
+    down_kept,
     h2_sum,
     out_sum,
     gu_sum,
@@ -1183,11 +1257,16 @@
     gu_quarter(p.r)
     for t in range(2 if p.n_hi > 2 else 1, p.n_hi):
         sums(t)
+    stores = Stores(pool)
+    stores.start(out_sum, out_kept)
+    stores.start(h2_sum, h2_kept)
     for b in down_blocks:
         down_rows.close(b)
+        stores.start(down_sum.at[b], down_kept.at[b])
     for b in gu_blocks:
         gu_rows.close(b)
-    for member in h2_parts + out_parts + [gu_rows, down_rows]:
+        stores.start(gu_sum.at[b], gu_kept.at[b])
+    for member in h2_parts + out_parts + [gu_rows, down_rows, stores]:
         member.finish()
 
 
@@ -1219,7 +1298,8 @@
     part = shape_of((seqs, tokens, width))
     shapes = (shape_of((tokens, width), f32), shape_of((tokens, width), f32), shape_of(gu_dims), shape_of(down_dims))
     scratch = (
-        [pltpu.VMEM(array.shape, low) for array in (h2, wgu, wdown, g)]
+        [pltpu.VMEM(member.shape, member.dtype) for member in shapes]
+        + [pltpu.VMEM(array.shape, low) for array in (h2, wgu, wdown, g)]
         + [pltpu.VMEM((row_tokens, hidden_own), low), pltpu.VMEM((row_tokens, 2 * hidden_own), low)]
         + [pltpu.VMEM(part.shape, low)]
         + seq_slots(part)
@@ -1234,7 +1314,7 @@
         4,
         (h2, wgu, wdown, g),
         [pl.ANY] * 4,
-        (pltpu.VMEM,) * 4,
+        (pl.ANY,) * 4,
         scratch,
         320,
     )
@@ -1246,9 +1326,9 @@
         n = place.seq_count
         self.own, self.send, self.recv = sems.take(1), sems.take(n), sems.take(n)
 
-    def start(self):
+    def start(self, first=0, last=None):
         p, s = self.p, self.p.s
-        for step in range(p.seq_count):
+        for step in range(first, p.seq_count if last is None else last):
             t = p.peer(step)
             piece = self.piece(t)
             for offset, width, target in self.parts(s):
@@ -1293,22 +1373,41 @@
         dqkv[:, lanes] = (dq_turned[...].T * scale).astype(jnp.bfloat16)
 
 
+def middle_back(middle, h2_grad, g, gain, middle_grad, branch, gain_part):
+    gain_part[...] = jnp.zeros_like(gain_part)
+
+    @pl.loop(0, middle.shape[0] // 16)
+    def _(tile):
+        rows = rows_at(tile, 16)
+        values, grads = middle[rows, :], h2_grad[rows, :]
+        inverse = lax.rsqrt(jnp.mean(values * values, axis=-1, keepdims=True) + EPSILON)
+        terms = grads * values * inverse
+        gain_part[...] += terms[:8] + terms[8:]
+        scaled = gain[...] * grads
+        total = (
+            g[rows, :].astype(jnp.float32)
+            + inverse * scaled
+            - values * inverse**3 * jnp.mean(scaled * values, axis=-1, keepdims=True)
+        )
+        middle_grad[rows, :] = total
+        branch[rows, :] = total.astype(branch.dtype)
+
+
 def back_kernel(
     rows,
     seqs,
     head_size,
-    do_own,
+    middle,
+    h2_grad,
+    g,
+    attended,
+    gain_values,
+    lengths,
+    gu,
+    wout_in,
     qkv_in,
     hn_in,
     wqkv_in,
-    out_in,
-    gu,
-    gain_two_part,
-    gain_one,
-    key_place,
-    query_low,
-    query_high,
-    shift,
     hn_sum,
     out_sum,
     query_got,
@@ -1317,10 +1416,10 @@
     gate_got,
     up_got,
     gain_got,
+    middle_kept,
     do,
     dqkv,
     dq_turned,
-    hn_part,
     hn_side,
     hn_chain,
     grad_qkv,
@@ -1336,24 +1435,28 @@
     qkv,
     hn,
     wqkv,
-    out_own,
+    wout,
+    out,
+    do_own,
+    branch,
+    middle_grad,
+    key_place,
+    query_low,
+    query_high,
+    shift,
     loads,
     sems,
 ):
     p, pool = Place(rows, seqs), Sems(sems)
-    pairs = (
-        (qkv_in, qkv),
-        (out_in.at[p.r_y], out_own.at[0]),
-        (wqkv_in, wqkv),
-        (hn_in, hn),
-        (out_in.at[p.r], out_own.at[1]),
-    )
+    pairs = ((wout_in, wout), (qkv_in, qkv), (wqkv_in, wqkv), (hn_in, hn))
     for number, (source, target) in enumerate(pairs):
         pltpu.make_async_copy(source, target, loads.at[number]).start()
     greet(p.peers() + p.rows())
+    stores = Stores(pool)
     tokens, own_width = do.shape
     block_tokens = tokens // seqs
     width = wqkv.shape[0]
+    hn_part = wout.at[pl.ds(0, tokens), :].reshape(seqs, block_tokens, width)
 
     def block_rows(b):
         return pl.ds(pl.multiple_of(b * block_tokens, block_tokens), block_tokens)
@@ -1361,19 +1464,16 @@
     do_swap = SeqExchange(
         p, pool, lambda t: columns(do_own, t, own_width), lambda b: do.at[block_rows(b), :]
     )
-    do_swap.start()
+    deep = width // (rows * seqs)
     out_rows = RowReduce(
         p,
         pool,
         seqs,
-        lambda r, b: out_in.at[r, b],
+        lambda r, b: out.at[pl.ds(pl.multiple_of((r * seqs + b) * deep, deep), deep), :],
         lambda w, b: out_core.at[w, b],
         lambda b: out_y.at[b],
         lambda b: out_y.at[b],
-        own=lambda w, b: out_own.at[w, b],
-    )
-    for b in range(seqs):
-        out_rows.start(b)
+    )
     hidden_own = gu.shape[2] // 2
     block = hidden_own // rows
 
@@ -1410,20 +1510,45 @@
         p, pool, lambda t: columns(gain_y, t // 2, gain_width), lambda b: gain_got.at[b]
     )
 
+    gu_swap.start(0, 3)
+    middle_back(middle, h2_grad, g, gain_values.at[4:5, :], middle_grad, branch, gains.at[8:16, :])
+    stores.start(middle_grad, middle_kept)
+    settle(wout, loads.at[0])
+
+    @pl.loop(0, width // 512)
+    def _(c):
+        lanes = rows_at(c, 512)
+        do_own[:, lanes] = nt(branch[...], wout[lanes, :]).astype(jnp.bfloat16)
+
+    do_swap.start()
+
+    def out_quarter(r):
+        @pl.loop(0, 2)
+        def _(c):
+            lanes = rows_at(2 * r + c, width // (2 * rows))
+            out[lanes, :] = tn(attended[:, lanes], branch[...]).astype(jnp.bfloat16)
+
+    out_quarter(p.r_far)
+    for b in range(seqs):
+        out_rows.start_far(b)
+    out_quarter(p.r_y)
+    out_quarter(p.r_core)
+    for b in range(seqs):
+        out_rows.start_core(b)
+    fill_meta(lengths, key_place, query_low, query_high, shift, block_tokens, seqs)
+    for b in range(seqs):
+        out_rows.step(b)
     for step in range(1, seqs):
         do_swap.step(step)
     settle(do.at[block_rows(p.s), :], do_swap.own(0))
-    gu_swap.start()
-    settle(out_own.at[0], loads.at[1])
-    for b in range(seqs):
-        out_rows.step(b)
-    settle(qkv, loads.at[0])
+    gu_swap.start(3, seqs)
+    out_quarter(p.r)
+    settle(qkv, loads.at[1])
     attention_back(qkv, do, dqkv, key_place, query_low, query_high, shift, dq_turned, head_size)
 
-    for number in (2, 3, 4):
+    for number in (2, 3):
         settle(pairs[number][1], loads.at[number])
     gains[0:8, :] = jnp.zeros_like(gains[0:8, :])
-    gains[8:16, :] = gain_two_part[...]
     column_step = 512
     for t in range(p.n_hi):
         pair = hn_parts[0].turn(t)
@@ -1440,7 +1565,7 @@
 
         for member in hn_parts:
             member.start(t)
-    gains[0:8, :] = gains[0:8, :] / gain_one[...]
+    gains[0:8, :] = gains[0:8, :] / gain_values[0:1, :]
     gain_rows.start(0)
 
     @pl.loop(0, width // 256)
@@ -1476,63 +1601,58 @@
     for step in range(1, seqs):
         gain_swap.step(step)
         settle(do.at[block_rows(p.s), :], do_swap.send(step))
-    for member in hn_parts + [out_rows, qkv_rows, gain_rows, gu_swap, qkv_swap, out_seq, gain_swap]:
+    for member in hn_parts + [out_rows, qkv_rows, gain_rows, gu_swap, qkv_swap, out_seq, gain_swap, stores]:
         member.finish()
 
 
-def back(rows, seqs, head_size, do_own, qkv, hn, wqkv, out, gu, gain_two_part, gain_one, meta):
+def back(rows, seqs, head_size, middle, h2_grad, g, attended, gain_values, lengths, gu, wout, qkv, hn, wqkv):
     tokens, own_width = qkv.shape[0], qkv.shape[1] // 3
     width = hn.shape[1]
-    low = jnp.bfloat16
-    out = row_blocks(rows, out, seqs)
+    low, f32 = jnp.bfloat16, jnp.float32
     block_tokens = tokens // seqs
-    hn_dims, qkv_dims = (seqs, block_tokens, width), (rows, seqs, width // (rows * seqs), 3 * own_width)
     deep = width // (rows * seqs)
     quarter = width // rows
+    hn_dims, qkv_dims = (seqs, block_tokens, width), (rows, seqs, deep, 3 * own_width)
     got = shape_of((deep, width))
     gu_got = shape_of((deep, gu.shape[2] // 2 * seqs))
     gain_width = 2 * quarter // seqs
     shapes = (
-        shape_of(hn_dims[1:], jnp.float32),
-        shape_of(out.shape[2:]),
+        shape_of(hn_dims[1:], f32),
+        got,
         got,
         got,
         got,
         gu_got,
         gu_got,
-        shape_of((seqs, 16, gain_width), jnp.float32),
-    )
-    hn_like, qkv_like, out_like = shape_of(hn_dims), shape_of(qkv_dims), shape_of(out.shape)
+        shape_of((seqs, 16, gain_width), f32),
+        shape_of(hn_dims[1:], f32),
+    )
+    qkv_like, out_like = shape_of(qkv_dims), shape_of((rows, seqs, deep, width))
     scratch = (
         [
             pltpu.VMEM((tokens, own_width), low),
             pltpu.VMEM(qkv.shape, low),
-            pltpu.VMEM((head_size, tokens), jnp.float32),
-            pltpu.VMEM(hn_dims, low),
+            pltpu.VMEM((head_size, tokens), f32),
         ]
-        + seq_slots(hn_like)
+        + seq_slots(shape_of(hn_dims))
         + [pltpu.VMEM(qkv_dims, low)]
         + row_slots(qkv_like)
         + row_slots(out_like)
-        + seq_slots(shape_of(out.shape[1:]))
-        + [
-            pltpu.VMEM((16, width), jnp.float32),
-            pltpu.VMEM((2, 16, quarter), jnp.float32),
-            pltpu.VMEM((16, quarter), jnp.float32),
-            pltpu.VMEM(qkv.shape, low),
-            pltpu.VMEM(hn.shape, low),
-            pltpu.VMEM(wqkv.shape, low),
-            pltpu.VMEM((2,) + out.shape[1:], low),
-            pltpu.SemaphoreType.DMA((5,)),
-        ]
+        + seq_slots(shape_of(out_like.shape[1:]))
+        + [pltpu.VMEM((16, width), f32), pltpu.VMEM((2, 16, quarter), f32), pltpu.VMEM((16, quarter), f32)]
+        + [pltpu.VMEM(array.shape, low) for array in (qkv, hn, wqkv, wout)]
+        + [pltpu.VMEM((width, width), low)]
+        + [pltpu.VMEM(hn_dims[1:], low), pltpu.VMEM(hn_dims[1:], low), pltpu.VMEM(hn_dims[1:], f32)]
+        + meta_scratch(tokens)
+        + [pltpu.SemaphoreType.DMA((4,))]
     )
     return call(
         functools.partial(back_kernel, rows, seqs, head_size),
         shapes,
         6,
-        (do_own, qkv, hn, wqkv, out, gu, gain_two_part, gain_one) + meta,
-        [pltpu.VMEM] + [pl.ANY] * 4 + [pltpu.VMEM] * 7,
-        (pltpu.VMEM,) * 5 + (pl.ANY,) * 2 + (pltpu.VMEM,),
+        (middle, h2_grad, g, attended, gain_values, lengths, gu, wout, qkv, hn, wqkv),
+        [pltpu.VMEM] * 5 + [pltpu.SMEM, pltpu.VMEM] + [pl.ANY] * 4,
+        (pltpu.VMEM,) * 5 + (pl.ANY,) * 2 + (pltpu.VMEM, pl.ANY),
         scratch,
         480,
     )
@@ -1575,24 +1695,6 @@
     gains_own = jnp.where(lane // deep == side, jnp.where(number < 4, both[0], both[1]), 0.0)
     x_low, g_low = inputs[0], cotangent[0]
 
-    def places(shape, axis):
-        index = lax.broadcasted_iota(jnp.int32, shape, axis)
-        block, within = index // tokens, lax.rem(index, tokens)
-        segment = position = length_of = jnp.zeros_like(index)
-        begin = 0
-        for n in range(lengths.shape[1]):
-            unit = lengths[0, n] // (2 * seqs)
-            inside = (within >= begin) & (within < begin + 2 * unit)
-            local = within - begin
-            here = jnp.where(local < unit, block * unit + local, (2 * seqs - 1 - block) * unit + local - unit)
-            segment = jnp.where(inside, n, segment)
-            position = jnp.where(inside, here, position)
-            length_of = jnp.where(inside, lengths[0, n], length_of)
-            begin = begin + 2 * unit
-        return segment * row_tokens, segment * row_tokens + position, length_of
-
-    query_low, query_high, length_of = places((1, row_tokens), 1)
-    meta = (places((row_tokens, 1), 0)[1], query_low, query_high, jnp.log(length_of.astype(f32)))
     g_all, wgu, wdown, wout, h2, wqkv, hn, qkv, attended, middle, gains = forward(
         rows,
         seqs,
@@ -1604,9 +1706,9 @@
         w_down,
         w_out,
         gains_own,
-        meta,
-    )
-    gain_one, gain_two = gains[0:1], gains[4:5]
+        lengths,
+    )
+    gain_one = gains[0:1]
     wqkv = wqkv.reshape(width, 3 * own_width)
     wgu = wgu.reshape(width, 2 * hidden_own)
     wdown = wdown.reshape(hidden_own, width)
@@ -1617,19 +1719,8 @@
     h2_grad, out_sum, sum_gu, sum_down = ffn(rows, seqs, h2, wgu, wdown, g_all)
     output = (middle + out_sum).astype(low)
 
-    inverse = lax.rsqrt(jnp.mean(middle * middle, axis=-1, keepdims=True) + EPSILON)
-    scaled_grad = gain_two * h2_grad
-    gain_two_part = jnp.sum((h2_grad * middle * inverse).reshape(-1, 8, width), axis=0)
-    middle_grad = (
-        g_low.astype(f32)
-        + inverse * scaled_grad
-        - middle * inverse**3 * jnp.mean(scaled_grad * middle, axis=-1, keepdims=True)
-    )
-    branch = middle_grad.astype(low)
-    grad_out = dot(attended, branch, 0, 0).astype(low)
-    do_own = dot(branch, wout, 1, 1).astype(low)
-    hn_grad, sum_out, got_query, got_key, got_value, got_gate, got_up, got_gain = back(
-        rows, seqs, head_size, do_own, qkv, hn, wqkv, grad_out, sum_gu, gain_two_part, gain_one, meta
+    hn_grad, sum_out, got_query, got_key, got_value, got_gate, got_up, got_gain, middle_grad = back(
+        rows, seqs, head_size, middle, h2_grad, g_low, attended, gains, lengths, sum_gu, wout, qkv, hn, wqkv
     )
     spread_inverse = lax.rsqrt(jnp.mean(residual * residual, axis=-1, keepdims=True) + EPSILON)
     scaled_grad = gain_one * hn_grad

time: 553 us -> 503 us (0.910)
  Pallas kernels: 504 us -> 480 us
  matrix products: 9.31 us -> 0 us
  other arithmetic: 22.2 us -> 13.3 us
    pallas_call x3, Pallas kernels: 504 us -> 480 us  [call(): pl.pallas_call(kernel, out_shape=shapes, in_specs=[pl.BlockSpec(memory_sp...]
    dot_general x2 -> x0, matrix products: 9.31 us -> none  [dot(): lax.dot_general(left, right, (((left_axis,), (right_axis,)), ((), ())), p...]
where the time goes in v1:
time: 503 us; the launch traced here: 497 us
  Pallas kernels  480 us (95%)
  other arithmetic  13.3 us (3%)
    pallas_call x3, Pallas kernels, call(): pl.pallas_call(kernel, out_shape=shapes, in_specs=[pl.BlockSpec(memory_sp...  480 us

profile of v1, /device:TPU:0, one launch (start us, length us, event | category | flops | bytes accessed | tf_op | source)
XLA Modules:
  0.0 496.5 jit_solution(9295629574143899275)
XLA Ops:
  0.7 0.8 maximum_convert_fusion
  1.5 0.7 select_select_fusion.gains
  2.2 220.6 %shard_map.203 = (bf16[8,128,2048]{2,1,0:T(8,128)(2,1)}, bf16[4,8,64,2048]{3,2,1,0:T(8,128)(2,1)}, bf16[4,4,64,2048]{3,2,1,0:T(8,128)(2,1)}, bf16[4,8,64,2048]{3...) custom-call(bf16[128,2048]{1,0:T(8,128)(2,1)} %bitcast.26, ...), custom_call_target="tpu_custom_call" | custom-call | tf_op jit(solution)/shard_map/pallas_call | solution.py:732
  222.8 116.1 %shard_map.204 = (f32[128,2048]{1,0:T(8,128)}, f32[128,2048]{1,0:T(8,128)}, bf16[8,64,2048]{2,1,0:T(8,128)(2,1)}, bf16[4,64,2048]{2,1,0:T(8,128)(2,1)}) custom-call(bf16[1024,2048]{1,0:T(8,128)(2,1)} %bitcast.29, bf16[2048,2048]{1,0:T(8,128)(2,1)} %bitcast.25, bf16[1024,2048]{1,0:T(8,128)(2,1)} %bitcast.28, bf16[1024,2048]{1,0:T(8,128)(2,1)} %bitcast.27), custom_call_target="tpu_custom_call" | custom-call | tf_op jit(solution)/shard_map/pallas_call | solution.py:732
  338.9 143.7 %shard_map.205 = (f32[128,2048]{1,0:T(8,128)}, bf16[64,2048]{1,0:T(8,128)(2,1)}, bf16[64,2048]{1,0:T(8,128)(2,1)}, bf16[64,2048]{1,0:T(8,128)(2,1)}, bf16[64,204...) custom-call(f32[128,2048]{1,0:T(8,128)} %get-tuple-element.35.middle, ...), custom_call_target="tpu_custom_call" | custom-call | tf_op jit(solution)/shard_map/pallas_call | solution.py:732
  482.6 0.0 copy-start
  482.6 2.8 convert_element_type.52
  485.4 0.0 copy-done.5
  485.4 1.5 convert_element_type.53
  486.9 0.9 slice.11
  487.8 0.0 copy-done.2
  487.8 0.0 copy-start.8
  487.8 0.3 fusion
  488.1 0.0 copy-done.4
  488.1 0.0 copy-start.11
  488.2 1.3 fusion.3
  489.5 0.8 convert_element_type.48
  490.3 0.8 convert_element_type.49
  491.1 0.8 convert_element_type.50
  492.0 0.8 convert_element_type.51
  492.8 0.1 reshape.108
  492.9 0.5 dynamic-slice_bitcast_fusion
  493.5 1.6 bitcast_convert_fusion
  495.1 0.9 fusion.5
  (25 shorter events, 0.1 us)
Async XLA Ops:
  482.6 2.9 copy-start.5
  482.6 5.2 %copy-start = (bf16[1,128,2048]{2,1,0:T(8,128)(2,1)S(1)}, bf16[1,128,2048]{2,1,0:T(8,128)(2,1)}, u32[]{:S(2)}) copy-start(bf16[1,128,2048]{2,1,0:T(8,128)(2,1)} %param.12) | copy-start | bytes 1572868
  482.6 5.2 %copy-start.2 = (f32[128,2048]{1,0:T(8,128)S(1)}, f32[128,2048]{1,0:T(8,128)}, u32[]{:S(2)}) copy-start(f32[128,2048]{1,0:T(8,128)} %get-tuple-element.50) | copy-start | bytes 3145732
  485.4 2.7 copy-start.4
  486.9 2.6 copy-start.10
  486.9 3.4 copy-start.9
  487.8 3.3 copy-start.8
  488.1 3.9 copy-start.7
  488.1 4.7 copy-start.11
  488.2 5.3 %copy-start.3 = (bf16[4,64,2048]{2,1,0:T(8,128)(2,1)S(1)}, bf16[4,64,2048]{2,1,0:T(8,128)(2,1)}, u32[]{:S(2)}) copy-start(bf16[4,64,2048]{2,1,0:T(8,128)(2,1)} %get-tuple-element.58) | copy-start | bytes 3145732
  489.5 5.6 %copy-start.1 = (f32[128,2048]{1,0:T(8,128)S(1)}, f32[128,2048]{1,0:T(8,128)}, u32[]{:S(2)}) copy-start(f32[128,2048]{1,0:T(8,128)} %get-tuple-element.35.middle) | copy-start | bytes 3145732
  489.5 5.6 %copy-start.6 = (f32[128,2048]{1,0:T(8,128)S(1)}, f32[128,2048]{1,0:T(8,128)}, u32[]{:S(2)}) copy-start(f32[128,2048]{1,0:T(8,128)} %get-tuple-element.40) | copy-start | bytes 3145732

commit v2 on v1

--- a/solution.py
+++ b/solution.py
@@ -1658,10 +1658,44 @@
     )
 
 
-def dot(left, right, left_axis=1, right_axis=0):
-    return lax.dot_general(
-        left, right, (((left_axis,), (right_axis,)), ((), ())), preferred_element_type=jnp.float32
-    )
+def ending_kernel(
+    middle, out_sum, middle_grad, hn_grad, x, gain, query, key, value, out, gate, up, down, *results
+):
+    output, input_grad = results[:2]
+    for source, target in zip((query, key, value, out, gate, up, down), results[2:]):
+        target[...] = source[...].astype(target.dtype)
+    output[...] = (middle[...] + out_sum[...]).astype(output.dtype)
+    values = x[...].astype(jnp.float32)
+    inverse = lax.rsqrt(jnp.mean(values * values, axis=-1, keepdims=True) + EPSILON)
+    scaled = gain[...] * hn_grad[...]
+    input_grad[...] = (
+        middle_grad[...]
+        + inverse * scaled
+        - values * inverse**3 * jnp.mean(scaled * values, axis=-1, keepdims=True)
+    )
+
+
+def ending(middle, out_sum, middle_grad, hn_grad, x, gain, gradients):
+    steps = 4
+    f32 = jnp.float32
+
+    def blocks(array):
+        return pl.BlockSpec((array.shape[0] // steps, array.shape[1]), lambda n: (n, 0))
+
+    args = (middle, out_sum, middle_grad, hn_grad, x)
+    shapes = (shape_of(middle.shape), shape_of(middle.shape, f32)) + tuple(
+        shape_of(member.shape, f32) for member in gradients
+    )
+    return pl.pallas_call(
+        ending_kernel,
+        grid=(steps,),
+        out_shape=shapes,
+        in_specs=[blocks(member) for member in args]
+        + [pl.BlockSpec(gain.shape, lambda n: (0, 0))]
+        + [blocks(member) for member in gradients],
+        out_specs=tuple(blocks(member) for member in shapes),
+        compiler_params=pltpu.CompilerParams(vmem_limit_bytes=VMEM_BYTES),
+    )(*args, gain, *gradients)
 
 
 def split_local(
@@ -1715,33 +1749,27 @@
     wout = wout.reshape(width, width)
     g_all = g_all.reshape(row_tokens, width)
     h2 = h2.reshape(row_tokens, width)
-    residual = x_low.astype(f32)
     h2_grad, out_sum, sum_gu, sum_down = ffn(rows, seqs, h2, wgu, wdown, g_all)
-    output = (middle + out_sum).astype(low)
 
     hn_grad, sum_out, got_query, got_key, got_value, got_gate, got_up, got_gain, middle_grad = back(
         rows, seqs, head_size, middle, h2_grad, g_low, attended, gains, lengths, sum_gu, wout, qkv, hn, wqkv
     )
-    spread_inverse = lax.rsqrt(jnp.mean(residual * residual, axis=-1, keepdims=True) + EPSILON)
-    scaled_grad = gain_one * hn_grad
-    input_grad = (
-        middle_grad
-        + spread_inverse * scaled_grad
-        - residual * spread_inverse**3 * jnp.mean(scaled_grad * residual, axis=-1, keepdims=True)
-    )
+    gradients = (got_query, got_key, got_value, sum_out, got_gate, got_up, sum_down.reshape(w_down.shape))
+    output, input_grad, *gradients = ending(middle, out_sum, middle_grad, hn_grad, x_low, gain_one, gradients)
     gain_sums = jnp.sum(got_gain, axis=0).reshape(2, 8, 2, deep).sum(axis=1)
     gain_sums = lax.dynamic_index_in_dim(gain_sums, lax.rem(lax.axis_index("seq"), 2), 1, keepdims=False)
+    grad_query, grad_key, grad_value, grad_out, grad_gate, grad_up, grad_down = gradients
     return (
         output[None],
         input_grad[None],
-        got_query.astype(f32),
-        got_key.astype(f32),
-        got_value.astype(f32),
-        sum_out.astype(f32),
+        grad_query,
+        grad_key,
+        grad_value,
+        grad_out,
         gain_sums[0],
-        got_gate.astype(f32),
-        got_up.astype(f32),
-        sum_down.reshape(w_down.shape).astype(f32),
+        grad_gate,
+        grad_up,
+        grad_down,
         gain_sums[1],
     )
 

time: 503 us -> 499 us (level)
  other arithmetic: 13.3 us -> 1.53 us
  Pallas kernels: 480 us -> 488 us
    convert_element_type x7 -> x0, other arithmetic: 9.24 us -> none  [the longest x1 2.83 us: split_local(): got_gate.astype(f32)]
    pallas_call x0 -> x1, Pallas kernels: none -> 7.64 us  [ending(): pl.pallas_call(ending_kernel, grid=(steps,), out_shape=shapes, in_specs=[...]
where the time goes in v2:
time: 499 us; the launch traced here: 492 us
  Pallas kernels  488 us (98%)
    pallas_call x3, Pallas kernels, call(): pl.pallas_call(kernel, out_shape=shapes, in_specs=[pl.BlockSpec(memory_sp...  480 us

profile of v2, /device:TPU:0, one launch (start us, length us, event | category | flops | bytes accessed | tf_op | source)
XLA Modules:
  0.0 492.5 jit_solution(6354895983691777560)
XLA Ops:
  0.7 0.8 maximum_convert_fusion
  1.5 0.7 select_select_fusion.gains
  2.2 220.6 %shard_map.203 = (bf16[8,128,2048]{2,1,0:T(8,128)(2,1)}, bf16[4,8,64,2048]{3,2,1,0:T(8,128)(2,1)}, bf16[4,4,64,2048]{3,2,1,0:T(8,128)(2,1)}, bf16[4,8,64,2048]{3...) custom-call(bf16[128,2048]{1,0:T(8,128)(2,1)} %bitcast.24, ...), custom_call_target="tpu_custom_call" | custom-call | tf_op jit(solution)/shard_map/pallas_call | solution.py:732
  222.8 116.1 %shard_map.204 = (f32[128,2048]{1,0:T(8,128)}, f32[128,2048]{1,0:T(8,128)}, bf16[8,64,2048]{2,1,0:T(8,128)(2,1)}, bf16[4,64,2048]{2,1,0:T(8,128)(2,1)}) custom-call(bf16[1024,2048]{1,0:T(8,128)(2,1)} %bitcast.20, bf16[2048,2048]{1,0:T(8,128)(2,1)} %bitcast.17, bf16[1024,2048]{1,0:T(8,128)(2,1)} %bitcast.19, bf16[1024,2048]{1,0:T(8,128)(2,1)} %bitcast.18), custom_call_target="tpu_custom_call" | custom-call | tf_op jit(solution)/shard_map/pallas_call | solution.py:732
  338.9 143.4 %shard_map.205 = (f32[128,2048]{1,0:T(8,128)}, bf16[64,2048]{1,0:T(8,128)(2,1)}, bf16[64,2048]{1,0:T(8,128)(2,1)}, bf16[64,2048]{1,0:T(8,128)(2,1)}, bf16[64,204...) custom-call(f32[128,2048]{1,0:T(8,128)} %get-tuple-element.44.middle, ...), custom_call_target="tpu_custom_call" | custom-call | tf_op jit(solution)/shard_map/pallas_call | solution.py:732
  482.3 1.4 slice.11.gain
  483.7 0.0 copy-start
  483.7 7.6 %shard_map.206 = (bf16[128,2048]{1,0:T(8,128)(2,1)}, f32[128,2048]{1,0:T(8,128)}, f32[64,2048]{1,0:T(8,128)}, f32[64,2048]{1,0:T(8,128)}, f32[64,2048]{1,0:T(8,1...) custom-call(f32[128,2048]{1,0:T(8,128)} %get-tuple-element.44.middle, ...), custom_call_target="tpu_custom_call" | custom-call | tf_op jit(solution)/shard_map/pallas_call | solution.py:1689
  491.4 0.0 copy-done
  491.4 0.1 reshape.91
  491.5 0.5 dynamic-slice_bitcast_fusion
  (5 shorter events, 0.1 us)
Async XLA Ops:
  483.7 7.7 %copy-start = (f32[8,16,128]{2,1,0:T(8,128)S(1)}, f32[8,16,128]{2,1,0:T(8,128)}, u32[]{:S(2)}) copy-start(f32[8,16,128]{2,1,0:T(8,128)} %get-tuple-element.73) | copy-start | bytes 196612

commit v3 on v2

--- a/solution.py
+++ b/solution.py
@@ -500,12 +500,15 @@
         s = self.p.s
         pltpu.make_async_copy(self.piece(s), self.at(s), self.own(0)).start()
 
+    def start_one(self, step):
+        p, s = self.p, self.p.s
+        t = p.peer(step)
+        push(self.piece(t), self.at(s), self.send(step), self.recv(s), (p.r, t))
+
     def start(self):
-        p, s = self.p, self.p.s
         self.start_own()
-        for step in range(1, p.seq_count):
-            t = p.peer(step)
-            push(self.piece(t), self.at(s), self.send(step), self.recv(s), (p.r, t))
+        for step in range(1, self.p.seq_count):
+            self.start_one(step)
 
     def step(self, step):
         block = self.p.peer(self.p.seq_count - step)
@@ -605,7 +608,10 @@
         return self.chain_slot(jnp.where(block == hi, self.p.n_hi, block))
 
     def turn(self, t):
-        p = self.p
+        return self.turn_of(self.p, t)
+
+    @staticmethod
+    def turn_of(p, t):
         n, hi = p.n_hi, p.hi
         low = jnp.where(t < n - 1 - hi, n - 1 - t, t - (n - 1 - hi))
         high = jnp.where(t < hi, t, n - 1 - (t - hi))
@@ -1134,11 +1140,16 @@
     sems,
 ):
     p, pool = Place(rows, seqs), Sems(sems)
-    pairs = ((h2_in, h2), (gu_in, gu_weights), (g_in, g), (down_in, down_weights))
-    for number, (source, target) in enumerate(pairs):
+    tokens, width = h2_sum.shape
+    turns = [SeqReduce.turn_of(p, t) for t in range(p.n_hi)]
+    talls = [rows_at(turn, 2 * tokens) for turn in turns]
+    pairs = [(gu_in, gu_weights), (down_in, down_weights)]
+    for tall in talls:
+        pairs += [(h2_in.at[tall, :], h2.at[tall, :]), (g_in.at[tall, :], g.at[tall, :])]
+    for number in [2, 0, 3, *(1, *range(4, len(pairs)))]:
+        source, target = pairs[number]
         pltpu.make_async_copy(source, target, loads.at[number]).start()
     greet(p.chain() + p.rows())
-    tokens, width = h2_sum.shape
     hidden_own = hidden.shape[1]
     low = jnp.bfloat16
     h2_parts = seq_reducers(p, pool, h2_part, h2_side, h2_chain, h2_sum)
@@ -1163,10 +1174,12 @@
         lambda b: down_sum.at[b],
         lambda b: down_sum.at[b],
     )
-    for number, (source, target) in enumerate(pairs):
-        settle(target, loads.at[number])
+    for number in range(2):
+        settle(pairs[number][1], loads.at[number])
 
     def products(t):
+        for number in (2 + 2 * t, 3 + 2 * t):
+            settle(pairs[number][1], loads.at[number])
         tall = rows_at(h2_parts[0].turn(t), 2 * tokens)
 
         @pl.loop(0, hidden_own // 256)
@@ -1306,7 +1319,7 @@
         + [pltpu.VMEM(part.shape, low)]
         + seq_slots(part)
         + [pltpu.VMEM((2,) + gu_dims, low), pltpu.VMEM((2,) + down_dims, low)]
-        + [pltpu.SemaphoreType.DMA((4,))]
+        + [pltpu.SemaphoreType.DMA((2 + seqs,))]
     )
     return call(
         functools.partial(ffn_kernel, rows, seqs),
@@ -1515,12 +1528,10 @@
     stores.start(middle_grad, middle_kept)
     settle(wout, loads.at[0])
 
-    @pl.loop(0, width // 512)
-    def _(c):
-        lanes = rows_at(c, 512)
+    for step in [*range(1, seqs), 0]:
+        lanes = rows_at(p.peer(step), own_width)
         do_own[:, lanes] = nt(branch[...], wout[lanes, :]).astype(jnp.bfloat16)
-
-    do_swap.start()
+        do_swap.start_one(step) if step else do_swap.start_own()
 
     def out_quarter(r):
         @pl.loop(0, 2)
@@ -1667,7 +1678,7 @@
     output[...] = (middle[...] + out_sum[...]).astype(output.dtype)
     values = x[...].astype(jnp.float32)
     inverse = lax.rsqrt(jnp.mean(values * values, axis=-1, keepdims=True) + EPSILON)
-    scaled = gain[...] * hn_grad[...]
+    scaled = gain[0:1, :] * hn_grad[...]
     input_grad[...] = (
         middle_grad[...]
         + inverse * scaled
@@ -1742,7 +1753,6 @@
         gains_own,
         lengths,
     )
-    gain_one = gains[0:1]
     wqkv = wqkv.reshape(width, 3 * own_width)
     wgu = wgu.reshape(width, 2 * hidden_own)
     wdown = wdown.reshape(hidden_own, width)
@@ -1755,7 +1765,7 @@
         rows, seqs, head_size, middle, h2_grad, g_low, attended, gains, lengths, sum_gu, wout, qkv, hn, wqkv
     )
     gradients = (got_query, got_key, got_value, sum_out, got_gate, got_up, sum_down.reshape(w_down.shape))
-    output, input_grad, *gradients = ending(middle, out_sum, middle_grad, hn_grad, x_low, gain_one, gradients)
+    output, input_grad, *gradients = ending(middle, out_sum, middle_grad, hn_grad, x_low, gains, gradients)
     gain_sums = jnp.sum(got_gain, axis=0).reshape(2, 8, 2, deep).sum(axis=1)
     gain_sums = lax.dynamic_index_in_dim(gain_sums, lax.rem(lax.axis_index("seq"), 2), 1, keepdims=False)
     grad_query, grad_key, grad_value, grad_out, grad_gate, grad_up, grad_down = gradients

time: 499 us -> 504 us (1.010); the launches traced: 492 us -> 505 us
  Pallas kernels: 488 us -> 502 us
    pallas_call x3, Pallas kernels: 480 us -> 495 us  [call(): pl.pallas_call(kernel, out_shape=shapes, in_specs=[pl.BlockSpec(memory_sp...]
where the time goes in v3:
time: 504 us; the launch traced here: 505 us
  Pallas kernels  502 us (100%)
    pallas_call x3, Pallas kernels, call(): pl.pallas_call(kernel, out_shape=shapes, in_specs=[pl.BlockSpec(memory_sp...  495 us

profile of v3, /device:TPU:0, one launch (start us, length us, event | category | flops | bytes accessed | tf_op | source)
XLA Modules:
  0.0 505.3 jit_solution(3776888614873220609)
XLA Ops:
  0.7 0.8 maximum_convert_fusion
  1.5 0.7 select_select_fusion.gains
  2.2 220.6 %shard_map.203 = (bf16[8,128,2048]{2,1,0:T(8,128)(2,1)}, bf16[4,8,64,2048]{3,2,1,0:T(8,128)(2,1)}, bf16[4,4,64,2048]{3,2,1,0:T(8,128)(2,1)}, bf16[4,8,64,2048]{3...) custom-call(bf16[128,2048]{1,0:T(8,128)(2,1)} %bitcast.24, ...), custom_call_target="tpu_custom_call" | custom-call | tf_op jit(solution)/shard_map/pallas_call | solution.py:738
  222.8 128.0 %shard_map.204 = (f32[128,2048]{1,0:T(8,128)}, f32[128,2048]{1,0:T(8,128)}, bf16[8,64,2048]{2,1,0:T(8,128)(2,1)}, bf16[4,64,2048]{2,1,0:T(8,128)(2,1)}) custom-call(bf16[1024,2048]{1,0:T(8,128)(2,1)} %bitcast.20, bf16[2048,2048]{1,0:T(8,128)(2,1)} %bitcast.17, bf16[1024,2048]{1,0:T(8,128)(2,1)} %bitcast.19, bf16[1024,2048]{1,0:T(8,128)(2,1)} %bitcast.18), custom_call_target="tpu_custom_call" | custom-call | tf_op jit(solution)/shard_map/pallas_call | solution.py:738
  350.8 146.0 %shard_map.205 = (f32[128,2048]{1,0:T(8,128)}, bf16[64,2048]{1,0:T(8,128)(2,1)}, bf16[64,2048]{1,0:T(8,128)(2,1)}, bf16[64,2048]{1,0:T(8,128)(2,1)}, bf16[64,204...) custom-call(f32[128,2048]{1,0:T(8,128)} %get-tuple-element.44.middle, ...), custom_call_target="tpu_custom_call" | custom-call | tf_op jit(solution)/shard_map/pallas_call | solution.py:738
  496.7 0.0 copy-start
  496.7 7.7 %shard_map.206 = (bf16[128,2048]{1,0:T(8,128)(2,1)}, f32[128,2048]{1,0:T(8,128)}, f32[64,2048]{1,0:T(8,128)}, f32[64,2048]{1,0:T(8,128)}, f32[64,2048]{1,0:T(8,1...) custom-call(f32[128,2048]{1,0:T(8,128)} %get-tuple-element.44.middle, ...), custom_call_target="tpu_custom_call" | custom-call | tf_op jit(solution)/shard_map/pallas_call | solution.py:1700
  504.5 0.0 copy-done
  504.5 0.1 reshape.91
  504.6 0.5 dynamic-slice_bitcast_fusion
  (5 shorter events, 0.0 us)
Async XLA Ops:
  496.7 7.7 %copy-start = (f32[8,16,128]{2,1,0:T(8,128)S(1)}, f32[8,16,128]{2,1,0:T(8,128)}, u32[]{:S(2)}) copy-start(f32[8,16,128]{2,1,0:T(8,128)} %get-tuple-element.73) | copy-start | bytes 196612
